TPU v7x, 256 devices: a whole 4x4x8 slice. The times are simulated.
256 devices in a mesh: col: 8 (over x_lo, y), row: 32 (over z, x_hi, core).
Axes of the slice: x: 4 (x_hi: 2, x_lo: 2; x = x_hi * 2 + x_lo), y: 4, z: 8, core: 2. Of those that a mesh axis runs over, the one named last changes fastest.
Arguments:
- upper_blocks: float32 [16384, 1024], P('row', 'col'), may hold values from -40 to 40
- lower_blocks: float32 [16384, 1024], P('row', 'col'), may hold values from -40 to 40
Outputs:
- upper_rotated: float32 [16384, 1024], P('row', 'col')
- lower_rotated: float32 [16384, 1024], P('row', 'col')
All inputs are finite; a program needn't handle non-finite values.
Results may differ from a plain program's by a relative error of at most 0.0001.
Values sent between devices are 32-bit elements; how exact they have to be, the bound alone decides.
No kernel may reach another device: no remote copies, remote signals or barrier semaphores. Data moves between devices by JAX's collectives and lax.ppermute only.
A program may use at most 64 MiB of HBM per device.

v0:
```python
import jax
import jax.numpy as jnp
from jax import lax
from jax.sharding import PartitionSpec as P

ROUNDS = 2


def cut_along(value, dim, devices):
    lengths = value.shape
    tiles = value.reshape(*lengths[:dim], devices, lengths[dim] // devices, *lengths[dim + 1 :])
    return jnp.moveaxis(tiles, dim, 0)


def summed_on_arrival(value, axis, dim):
    devices = lax.axis_size(axis)
    tiles = lax.all_to_all(cut_along(value, dim, devices), axis, 0, 0, tiled=True)
    return jnp.sum(tiles, axis=0)


def from_everyone(value, axis):
    devices = lax.axis_size(axis)
    return lax.all_to_all(
        jnp.broadcast_to(value[None], (devices, *value.shape)), axis, 0, 0, tiled=True
    )


def over_copies(value, axis):
    return from_everyone(value, axis).sum(axis=0)


def in_order(tiles, dim):
    lengths = list(tiles.shape[1:])
    lengths[dim] *= tiles.shape[0]
    return jnp.moveaxis(tiles, 0, dim).reshape(lengths)


def collect(value, axis, dim):
    return in_order(from_everyone(value, axis), dim)


def from_behind(block, axis, distance):
    devices = range(lax.axis_size(axis))
    route = [((i - distance) % len(devices), i) for i in devices]
    return lax.ppermute(block, axis, route)


def couple(cross_gram, upper_norms, lower_norms):
    column_gap = upper_norms[..., :, None] - lower_norms[..., None, :]
    column_sum = upper_norms[..., :, None] + lower_norms[..., None, :]
    return (
        -cross_gram
        * column_gap
        / (2.0 * column_gap * column_gap + 0.5 * column_sum * column_sum + 1e-05)
    )


def rotation(coupling):
    identity = jnp.eye(coupling.shape[0], dtype=coupling.dtype)
    outer_gram = jnp.dot(coupling, coupling.T, precision=lax.Precision.HIGHEST)
    inner_gram = jnp.dot(coupling.T, coupling, precision=lax.Precision.HIGHEST)
    left_factor = jnp.linalg.cholesky(identity + outer_gram)
    right_factor = jnp.linalg.cholesky(identity + inner_gram)
    keep_upper = jax.scipy.linalg.cho_solve((left_factor, True), identity - outer_gram)
    upper_to_lower = jax.scipy.linalg.cho_solve((left_factor, True), 2.0 * coupling)
    lower_to_upper = jax.scipy.linalg.cho_solve((right_factor, True), -2.0 * coupling.T)
    keep_lower = jax.scipy.linalg.cho_solve((right_factor, True), identity - inner_gram)
    return (keep_upper, upper_to_lower, lower_to_upper, keep_lower)


def statistics(pieces):
    cross_gram = 0.0
    upper_sums = 0.0
    lower_sums = 0.0
    for entry in pieces:
        cross_gram = cross_gram + jnp.einsum(
            "rb,rd->bd", entry[0], entry[1], precision=lax.Precision.HIGHEST
        )
        upper_sums = upper_sums + jnp.sum(entry[0] * entry[0], axis=0)
        lower_sums = lower_sums + jnp.sum(entry[1] * entry[1], axis=0)
    return (cross_gram, upper_sums, lower_sums)


def rotate(first_part, second_part, from_first, from_second):
    highest = lax.Precision.HIGHEST
    return jnp.dot(first_part, from_first, precision=highest) + jnp.dot(
        second_part, from_second, precision=highest
    )


def shards(upper_blocks, lower_blocks):
    rows_dev = upper_blocks.shape[0]
    block_width = upper_blocks.shape[1]
    row_count = lax.axis_size("row")
    row_total = float(rows_dev * row_count)
    pieces = [(upper_blocks, lower_blocks)]
    for round_index in range(ROUNDS):
        cross_gram, upper_sums, lower_sums = statistics(pieces)
        shared_rows = summed_on_arrival(cross_gram, "row", 0)
        upper_sums, lower_sums = (over_copies(upper_sums, "row"), over_copies(lower_sums, "row"))
        share_rows = block_width // row_count
        first_row = lax.axis_index("row") * share_rows
        upper_share = lax.dynamic_slice_in_dim(upper_sums / row_total, first_row, share_rows)
        coupling_share = couple(shared_rows / row_total, upper_share, lower_sums / row_total)
        coupling = collect(coupling_share, "row", 0)
        keep_upper, upper_to_lower, lower_to_upper, keep_lower = rotation(coupling)
        turned = [
            (
                rotate(entry[0], entry[1], keep_upper, lower_to_upper),
                rotate(entry[0], entry[1], upper_to_lower, keep_lower),
            )
            for entry in pieces
        ]
        if round_index + 1 < ROUNDS:
            pieces = [(from_behind(turned[0][0], "col", 1), from_behind(turned[0][1], "col", -1))]
        else:
            pieces = turned
    upper_rotated = jnp.concatenate([entry[0] for entry in pieces], axis=0)
    lower_rotated = jnp.concatenate([entry[1] for entry in pieces], axis=0)
    return (upper_rotated, lower_rotated)


def solution(mesh):
    placed = (P("row", "col"), P("row", "col"))
    return jax.shard_map(
        shards,
        mesh=mesh,
        in_specs=placed,
        out_specs=(P("row", "col"), P("row", "col")),
        check_vma=False,
    )
```

profile of v0, /device:TPU:1, one launch (start us, length us, event | category | flops | bytes accessed | tf_op | source)
XLA Modules:
  0.0 245.9 jit_solution(14683434871713824166)
XLA Ops:
  0.6 1.1 multiply_reduce_fusion.3
  1.7 0.6 broadcast_in_dim.12
  2.4 12.6 %all-to-all-start.1 = ((f32[32,1,128]{2,1,0:T(1,128)}), f32[32,1,128]{2,1,0:T(1,128)S(1)}, u32[]{:S(2)}, u32[]{:S(2)}) async-start(f32[32,1,128]{2,1,0:T(1,128)} %broadcast_in_dim.12), calls=%async_computation.1 | async-start | bytes 32768 | tf_op jit(solution)/shard_map/all_to_all | solution.py:23
  15.0 2.2 fusion.64
  17.3 6.9 %all-to-all-done.1 = f32[32,1,128]{2,1,0:T(1,128)S(1)} async-done(((f32[32,1,128]{2,1,0:T(1,128)}), f32[32,1,128]{2,1,0:T(1,128)S(1)}, u32[]{:S(2)}, u32[]{:S(2)}) %all-to-all-start.1) | async-done | bytes 16416 | tf_op jit(solution)/shard_map/all_to_all | solution.py:23
  24.2 0.6 broadcast_in_dim.13
  24.8 4.1 %all-to-all-start.2 = ((f32[32,1,128]{2,1,0:T(1,128)}), f32[32,1,128]{2,1,0:T(1,128)S(1)}, u32[]{:S(2)}, u32[]{:S(2)}) async-start(f32[32,1,128]{2,1,0:T(1,128)} %broadcast_in_dim.13), calls=%async_computation.2 | async-start | bytes 32768 | tf_op jit(solution)/shard_map/all_to_all | solution.py:23
  29.0 9.4 %all-to-all-done.2 = f32[32,1,128]{2,1,0:T(1,128)S(1)} async-done(((f32[32,1,128]{2,1,0:T(1,128)}), f32[32,1,128]{2,1,0:T(1,128)S(1)}, u32[]{:S(2)}, u32[]{:S(2)}) %all-to-all-start.2) | async-done | bytes 16416 | tf_op jit(solution)/shard_map/all_to_all | solution.py:23
  38.4 4.1 %all-to-all-start = ((f32[32,4,128]{2,1,0:T(4,128)}), f32[32,4,128]{2,1,0:T(4,128)S(1)}, u32[]{:S(2)}, u32[]{:S(2)}) async-start(f32[32,4,128]{2,1,0:T(4,128)} %bitcast), calls=%async_computation | async-start | bytes 131072 | tf_op jit(solution)/shard_map/all_to_all | solution.py:17
  42.6 9.8 %all-to-all-done = f32[32,4,128]{2,1,0:T(4,128)S(1)} async-done(((f32[32,4,128]{2,1,0:T(4,128)}), f32[32,4,128]{2,1,0:T(4,128)S(1)}, u32[]{:S(2)}, u32[]{:S(2)}) %all-to-all-start) | async-done | bytes 65568 | tf_op jit(solution)/shard_map/all_to_all | solution.py:17
  52.5 12.9 %all_to_all.44 = f32[32,4,128]{2,1,0:T(4,128)S(1)} all-to-all(f32[32,4,128]{2,1,0:T(4,128)S(1)} %broadcast_in_dim.14), channel_id=1, replica_groups=mesh['col'=8,'row'=32] {'row'}, dimensions={0} | all-to-all | bytes 131072 | tf_op jit(solution)/shard_map/all_to_all | solution.py:23
  65.9 11.7 %cholesky.74 = f32[128,128]{1,0:T(8,128)S(1)} custom-call(f32[128,128]{1,0:T(8,128)S(1)} %fusion.43), custom_call_target="Cholesky" | custom-call | tf_op jit(solution)/shard_map/jit(cholesky)/cholesky | solution.py:62
  77.6 0.6 compare_reduce_fusion.3
  78.3 0.7 fusion.2
  78.9 9.8 %custom-call.14 = f32[1,128,128]{1,2,0:T(8,128)S(1)} custom-call(f32[1,128,128]{2,1,0:T(8,128)S(1)} %fusion.2), custom_call_target="InvertDiagBlocksLowerTriangular" | custom-call | tf_op jit(solution)/shard_map/jit(_cho_solve)/triangular_solve | solution.py:64
  89.7 11.7 %cholesky.85 = f32[128,128]{1,0:T(8,128)S(1)} custom-call(f32[128,128]{1,0:T(8,128)S(1)} %fusion.35), custom_call_target="Cholesky" | custom-call | tf_op jit(solution)/shard_map/jit(cholesky)/cholesky | solution.py:63
  101.5 0.6 compare_reduce_fusion.2
  102.1 0.7 fusion.3
  102.8 22.7 %custom-call.15 = f32[1,128,128]{1,2,0:T(8,128)S(1)} custom-call(f32[1,128,128]{2,1,0:T(8,128)S(1)} %fusion.3), custom_call_target="InvertDiagBlocksLowerTriangular" | custom-call | tf_op jit(solution)/shard_map/jit(_cho_solve)/triangular_solve | solution.py:66
  126.3 0.4 fusion.65
  127.0 0.4 fusion.1
  127.4 1.4 collective-permute-start
  129.0 0.4 fusion.66
  129.7 0.4 fusion
  130.1 2.4 collective-permute-start.1
  132.5 4.7 %collective-permute-done = f32[512,128]{0,1:T(8,128)S(1)} collective-permute-done((f32[512,128]{0,1:T(8,128)S(1)}, f32[512,128]{0,1:T(8,128)S(1)}, u32[]{:S(2)}, u32[]{:S(2)}) %collective-permute-start) | collective-permute-done | bytes 262176 | tf_op jit(solution)/shard_map/ppermute | solution.py:45
  137.2 0.6 broadcast_in_dim.15
  137.8 4.7 %all-to-all-start.5 = ((f32[32,1,128]{2,1,0:T(1,128)}), f32[32,1,128]{2,1,0:T(1,128)S(1)}, u32[]{:S(2)}, u32[]{:S(2)}) async-start(f32[32,1,128]{2,1,0:T(1,128)} %broadcast_in_dim.15), calls=%async_computation.5 | async-start | bytes 32768 | tf_op jit(solution)/shard_map/all_to_all | solution.py:23
  142.6 1.0 fusion.67
  143.7 8.3 %all-to-all-done.5 = f32[32,1,128]{2,1,0:T(1,128)S(1)} async-done(((f32[32,1,128]{2,1,0:T(1,128)}), f32[32,1,128]{2,1,0:T(1,128)S(1)}, u32[]{:S(2)}, u32[]{:S(2)}) %all-to-all-start.5) | async-done | bytes 16416 | tf_op jit(solution)/shard_map/all_to_all | solution.py:23
  152.0 0.6 broadcast_in_dim.16
  152.6 4.1 %all-to-all-start.6 = ((f32[32,1,128]{2,1,0:T(1,128)}), f32[32,1,128]{2,1,0:T(1,128)S(1)}, u32[]{:S(2)}, u32[]{:S(2)}) async-start(f32[32,1,128]{2,1,0:T(1,128)} %broadcast_in_dim.16), calls=%async_computation.6 | async-start | bytes 32768 | tf_op jit(solution)/shard_map/all_to_all | solution.py:23
  156.8 9.3 %all-to-all-done.6 = f32[32,1,128]{2,1,0:T(1,128)S(1)} async-done(((f32[32,1,128]{2,1,0:T(1,128)}), f32[32,1,128]{2,1,0:T(1,128)S(1)}, u32[]{:S(2)}, u32[]{:S(2)}) %all-to-all-start.6) | async-done | bytes 16416 | tf_op jit(solution)/shard_map/all_to_all | solution.py:23
  166.1 4.1 %all-to-all-start.4 = ((f32[32,4,128]{2,1,0:T(4,128)}), f32[32,4,128]{2,1,0:T(4,128)S(1)}, u32[]{:S(2)}, u32[]{:S(2)}) async-start(f32[32,4,128]{2,1,0:T(4,128)} %bitcast.20), calls=%async_computation.4 | async-start | bytes 131072 | tf_op jit(solution)/shard_map/all_to_all | solution.py:17
  170.2 9.9 %all-to-all-done.4 = f32[32,4,128]{2,1,0:T(4,128)S(1)} async-done(((f32[32,4,128]{2,1,0:T(4,128)}), f32[32,4,128]{2,1,0:T(4,128)S(1)}, u32[]{:S(2)}, u32[]{:S(2)}) %all-to-all-start.4) | async-done | bytes 65568 | tf_op jit(solution)/shard_map/all_to_all | solution.py:17
  180.3 12.9 %all_to_all.45 = f32[32,4,128]{2,1,0:T(4,128)S(1)} all-to-all(f32[32,4,128]{2,1,0:T(4,128)S(1)} %broadcast_in_dim.18), channel_id=1, replica_groups=mesh['col'=8,'row'=32] {'row'}, dimensions={0} | all-to-all | bytes 131072 | tf_op jit(solution)/shard_map/all_to_all | solution.py:23
  193.6 11.7 %cholesky.96 = f32[128,128]{1,0:T(8,128)S(1)} custom-call(f32[128,128]{1,0:T(8,128)S(1)} %fusion.26), custom_call_target="Cholesky" | custom-call | tf_op jit(solution)/shard_map/jit(cholesky)/cholesky | solution.py:62
  205.3 0.6 compare_reduce_fusion.1
  206.0 0.7 fusion.4
  206.6 9.8 %custom-call.18 = f32[1,128,128]{1,2,0:T(8,128)S(1)} custom-call(f32[1,128,128]{2,1,0:T(8,128)S(1)} %fusion.4), custom_call_target="InvertDiagBlocksLowerTriangular" | custom-call | tf_op jit(solution)/shard_map/jit(_cho_solve)/triangular_solve | solution.py:64
  217.5 11.7 %cholesky.107 = f32[128,128]{1,0:T(8,128)S(1)} custom-call(f32[128,128]{1,0:T(8,128)S(1)} %fusion.18), custom_call_target="Cholesky" | custom-call | tf_op jit(solution)/shard_map/jit(cholesky)/cholesky | solution.py:63
  229.2 0.6 compare_reduce_fusion
  229.9 0.7 fusion.5
  230.5 10.0 %custom-call.19 = f32[1,128,128]{1,2,0:T(8,128)S(1)} custom-call(f32[1,128,128]{2,1,0:T(8,128)S(1)} %fusion.5), custom_call_target="InvertDiagBlocksLowerTriangular" | custom-call | tf_op jit(solution)/shard_map/jit(_cho_solve)/triangular_solve | solution.py:66
  241.9 0.6 fusion.69
  242.5 0.6 fusion.68
  243.1 1.3 convolution_add_fusion
  244.4 1.3 convolution_add_fusion.1
  (56 shorter events, 6.4 us)
Async XLA Ops:
  0.6 14.3 %copy-start = (f32[512,128]{1,0:T(8,128)S(1)}, f32[512,128]{1,0:T(8,128)}, u32[]{:S(2)}) copy-start(f32[512,128]{1,0:T(8,128)} %param.5) | copy-start | bytes 786436
  2.4 21.9 %all-to-all-start.1 = ((f32[32,1,128]{2,1,0:T(1,128)}), f32[32,1,128]{2,1,0:T(1,128)S(1)}, u32[]{:S(2)}, u32[]{:S(2)}) async-start(f32[32,1,128]{2,1,0:T(1,128)} %broadcast_in_dim.12), calls=%async_computation.1 | async-start | bytes 32768 | tf_op jit(solution)/shard_map/all_to_all | solution.py:23
  15.0 2.2 copy-start.1
  24.8 13.5 %all-to-all-start.2 = ((f32[32,1,128]{2,1,0:T(1,128)}), f32[32,1,128]{2,1,0:T(1,128)S(1)}, u32[]{:S(2)}, u32[]{:S(2)}) async-start(f32[32,1,128]{2,1,0:T(1,128)} %broadcast_in_dim.13), calls=%async_computation.2 | async-start | bytes 32768 | tf_op jit(solution)/shard_map/all_to_all | solution.py:23
  38.4 14.0 %all-to-all-start = ((f32[32,4,128]{2,1,0:T(4,128)}), f32[32,4,128]{2,1,0:T(4,128)S(1)}, u32[]{:S(2)}, u32[]{:S(2)}) async-start(f32[32,4,128]{2,1,0:T(4,128)} %bitcast), calls=%async_computation | async-start | bytes 131072 | tf_op jit(solution)/shard_map/all_to_all | solution.py:17
  127.4 9.7 %collective-permute-start = (f32[512,128]{0,1:T(8,128)S(1)}, f32[512,128]{0,1:T(8,128)S(1)}, u32[]{:S(2)}, u32[]{:S(2)}) collective-permute-start(f32[512,128]{0,1:T(8,128)S(1)} %fusion.1), channel_id=1, source_target_pairs={{224,0},{0,32},{32,64},{64,96},{96,128},{128,160},{160,192},{192,2... | collective-permute-start | bytes 786440 | tf_op jit(solution)/shard_map/ppermute | solution.py:45
  130.1 12.5 %collective-permute-start.1 = (f32[512,128]{0,1:T(8,128)S(1)}, f32[512,128]{0,1:T(8,128)S(1)}, u32[]{:S(2)}, u32[]{:S(2)}) collective-permute-start(f32[512,128]{0,1:T(8,128)S(1)} %fusion), channel_id=1, source_target_pairs={{32,0},{64,32},{96,64},{128,96},{160,128},{192,160},{224,192},{0,2... | collective-permute-start | bytes 786440 | tf_op jit(solution)/shard_map/ppermute | solution.py:45
  137.8 14.1 %all-to-all-start.5 = ((f32[32,1,128]{2,1,0:T(1,128)}), f32[32,1,128]{2,1,0:T(1,128)S(1)}, u32[]{:S(2)}, u32[]{:S(2)}) async-start(f32[32,1,128]{2,1,0:T(1,128)} %broadcast_in_dim.15), calls=%async_computation.5 | async-start | bytes 32768 | tf_op jit(solution)/shard_map/all_to_all | solution.py:23
  152.6 13.5 %all-to-all-start.6 = ((f32[32,1,128]{2,1,0:T(1,128)}), f32[32,1,128]{2,1,0:T(1,128)S(1)}, u32[]{:S(2)}, u32[]{:S(2)}) async-start(f32[32,1,128]{2,1,0:T(1,128)} %broadcast_in_dim.16), calls=%async_computation.6 | async-start | bytes 32768 | tf_op jit(solution)/shard_map/all_to_all | solution.py:23
  166.1 14.0 %all-to-all-start.4 = ((f32[32,4,128]{2,1,0:T(4,128)}), f32[32,4,128]{2,1,0:T(4,128)S(1)}, u32[]{:S(2)}, u32[]{:S(2)}) async-start(f32[32,4,128]{2,1,0:T(4,128)} %bitcast.20), calls=%async_computation.4 | async-start | bytes 131072 | tf_op jit(solution)/shard_map/all_to_all | solution.py:17
where the time goes:
time: 249 us; the launch traced here: 246 us
  other arithmetic  106 us (43%)
  waiting for transfers between devices  58.3 us (23%)
  starting transfers between devices  37.4 us (15%)
  blocking collectives  25.9 us (10%)
  matrix products  13.7 us (6%)
  local copies, waits for them, and re-layouts  3.03 us (1%)
    another operation x4, other arithmetic, rotation(): jax.scipy.linalg.cho_solve((right_factor, True), -2.0 * coupling.T)  34 us
    all_to_all x4, waiting for transfers between devices, from_everyone(): lax.all_to_all(jnp.broadcast_to(value[None], (devices, *value.shape)), ax...  33.9 us
    all_to_all x2, blocking collectives, from_everyone(): lax.all_to_all(jnp.broadcast_to(value[None], (devices, *value.shape)), ax...  25.9 us
    all_to_all x4, starting transfers between devices, from_everyone(): lax.all_to_all(jnp.broadcast_to(value[None], (devices, *value.shape)), ax...  25.5 us
    another operation x6, other arithmetic, rotation(): right_factor = jnp.linalg.cholesky(identity + inner_gram)  24.8 us
    another operation x6, other arithmetic, rotation(): left_factor = jnp.linalg.cholesky(identity + outer_gram)  24.8 us
    another operation x4, other arithmetic, rotation(): jax.scipy.linalg.cho_solve((left_factor, True), identity - outer_gram)  20.9 us
    all_to_all x2, waiting for transfers between devices, summed_on_arrival(): lax.all_to_all(cut_along(value, dim, devices), axis, 0, 0, tiled=True)  19.7 us
  transfers between devices with their start and end apart: 8, of which 7 were waited for; matrix products, arithmetic and copies ran while one was open for 2% of the time, Pallas kernels for 0%

commit v1 on v0

v1 whole, which is shorter than its diff:
```python
import functools

import jax
import jax.numpy as jnp
from jax import lax
from jax.experimental import pallas as pl
from jax.experimental.pallas import tpu as pltpu
from jax.sharding import PartitionSpec as P

ROUNDS = 2
HALF_ROWS = 72
TOLERANCE = 1e-7

Z_PAIR = {0: 1, 2: 3, 4: 5, 6: 7}
Z_FAR = ({0: 2, 1: 3, 4: 6, 5: 7}, {0: 6, 1: 7, 2: 4, 3: 5}, {0: 5, 1: 4, 2: 7, 3: 6})


def both_ways(pairs):
    return {**pairs, **{b: a for a, b in pairs.items()}}


def row_route(z_map=None, flip_x=False, flip_core=False):
    route = []
    for i in range(32):
        z, x, core = i // 4, i // 2 % 2, i % 2
        z = both_ways(z_map)[z] if z_map else z
        route.append((i, z * 4 + (x ^ flip_x) * 2 + (core ^ flip_core)))
    return route


def across(value, **kinds):
    return lax.ppermute(value, "row", row_route(**kinds))


def summed_over_chips(value):
    near = [across(value, flip_x=True), across(value, z_map=Z_PAIR), across(value, z_map=Z_PAIR, flip_x=True)]
    value = (value + near[0]) + (near[1] + near[2])
    far = [across(value, z_map=pairs) for pairs in Z_FAR]
    return (value + far[0]) + (far[1] + far[2])


def split(value):
    high = value.astype(jnp.bfloat16)
    return high, (value - high.astype(jnp.float32)).astype(jnp.bfloat16)


def contract(a, b, dims):
    (ah, al), (bh, bl) = a, b
    dot = functools.partial(lax.dot_general, dimension_numbers=(dims, ((), ())), preferred_element_type=jnp.float32)
    return dot(ah, bh) + (dot(al, bh) + dot(ah, bl))


def exact_dot(a, b, dims=((1,), (0,))):
    return lax.dot_general(
        a, b, dimension_numbers=(dims, ((), ())), precision=lax.Precision.HIGHEST, preferred_element_type=jnp.float32
    )


def statistics_kernel(upper_ref, lower_ref, keep_ref, send_ref):
    core = lax.axis_index("row") % 2
    upper, lower = upper_ref[...], lower_ref[...]
    gram = contract(split(upper), split(lower), ((0,), (0,)))
    sums = [jnp.sum((v * v).reshape(-1, 8, v.shape[1]), axis=0) for v in (upper, lower)]
    mine = core == 0
    keep_ref[:64] = jnp.where(mine, gram[:64], gram[64:])
    send_ref[:64] = jnp.where(mine, gram[64:], gram[:64])
    keep_ref[64:] = jnp.where(mine, sums[0], sums[1])
    send_ref[64:] = jnp.where(mine, sums[1], sums[0])


def statistics(upper, lower):
    half = jax.ShapeDtypeStruct((HALF_ROWS, upper.shape[1]), jnp.float32)
    vmem = pl.BlockSpec(memory_space=pltpu.VMEM)
    return pl.pallas_call(
        statistics_kernel, out_shape=(half, half), in_specs=[vmem, vmem], out_specs=(vmem, vmem), name="statistics"
    )(upper, lower)


def rotate_kernel(row_total, mine_ref, other_ref, upper_ref, lower_ref, new_upper_ref, new_lower_ref, residual_ref, inverse_ref):
    core = lax.axis_index("row") % 2
    mine, other = mine_ref[...], other_ref[...]
    first = jnp.where(core == 0, mine, other)
    second = jnp.where(core == 0, other, mine)
    width = mine.shape[1]
    scale = 1.0 / row_total
    cross_gram = jnp.concatenate([first[:64], second[:64]], axis=0) * scale
    upper_norms = jnp.sum(first[64:], axis=0, keepdims=True) * scale
    lower_norms = jnp.sum(second[64:], axis=0, keepdims=True) * scale
    upper_norms = jnp.broadcast_to(upper_norms, (width, width)).T
    gap = upper_norms - lower_norms
    both = upper_norms + lower_norms
    coupling = -cross_gram * gap / (2.0 * gap * gap + 0.5 * both * both + 1e-05)

    identity = (
        lax.broadcasted_iota(jnp.int32, (width, width), 0) == lax.broadcasted_iota(jnp.int32, (width, width), 1)
    ).astype(jnp.float32)
    outer = exact_dot(coupling, coupling, ((1,), (1,)))
    size = jnp.sqrt(jnp.sum(jnp.sum(outer * outer, axis=0, keepdims=True), axis=1, keepdims=True))
    alpha = 2.0 / (2.0 + size)
    bound = jnp.sum(size / (2.0 + size))
    residual_ref[...] = (1.0 - alpha) * identity - alpha * outer
    inverse_ref[...] = alpha * (identity + residual_ref[...])

    def factor(bound):
        residual = exact_dot(residual_ref[...], residual_ref[...])
        residual_ref[...] = residual
        inverse_ref[...] += exact_dot(inverse_ref[...], residual)
        return bound * bound

    lax.while_loop(lambda bound: bound > TOLERANCE, factor, bound * bound)

    @pl.when(bound > 0.5)
    def _():
        for _ in range(2):
            value = inverse_ref[...]
            inverse_ref[...] = value + exact_dot(value, (identity - value) - exact_dot(outer, value))

    inverse = inverse_ref[...]
    across_parts = 2.0 * exact_dot(inverse, coupling)
    upper_loss = 2.0 * exact_dot(outer, inverse)
    lower_loss = exact_dot(coupling, across_parts, ((0,), (0,)))
    change = jnp.concatenate(
        [
            jnp.concatenate([-upper_loss, across_parts], axis=1),
            jnp.concatenate([-across_parts.T, -lower_loss], axis=1),
        ],
        axis=0,
    )
    upper, lower = upper_ref[...], lower_ref[...]
    moved = contract(split(jnp.concatenate([upper, lower], axis=1)), split(change), ((1,), (0,)))
    new_upper_ref[...] = upper + moved[:, :width]
    new_lower_ref[...] = lower + moved[:, width:]


def rotated(mine, other, upper, lower, row_total):
    vmem = pl.BlockSpec(memory_space=pltpu.VMEM)
    return pl.pallas_call(
        functools.partial(rotate_kernel, row_total),
        out_shape=(jax.ShapeDtypeStruct(upper.shape, jnp.float32),) * 2,
        in_specs=[vmem] * 4,
        out_specs=(vmem, vmem),
        scratch_shapes=[pltpu.VMEM((upper.shape[1],) * 2, jnp.float32)] * 2,
        name="rotate",
    )(mine, other, upper, lower)


def from_behind(block, distance):
    devices = lax.axis_size("col")
    return lax.ppermute(block, "col", [((i - distance) % devices, i) for i in range(devices)])


def shards(upper, lower):
    row_total = float(upper.shape[0] * lax.axis_size("row"))
    for round_index in range(ROUNDS):
        keep, send = statistics(upper, lower)
        mine = summed_over_chips(keep + across(send, flip_core=True))
        other = across(mine, flip_core=True)
        upper, lower = rotated(mine, other, upper, lower, row_total)
        if round_index + 1 < ROUNDS:
            upper, lower = from_behind(upper, 1), from_behind(lower, -1)
    return upper, lower


def solution(mesh):
    placed = (P("row", "col"), P("row", "col"))
    return jax.shard_map(shards, mesh=mesh, in_specs=placed, out_specs=placed, check_vma=False)
```

time: 249 us -> 80.6 us (0.32); the launches traced: 246 us -> 80.3 us
  other arithmetic: 106 us -> 1.59 us
  waiting for transfers between devices: 58.3 us -> 22.5 us
  blocking collectives: 25.9 us -> 0 us
  Pallas kernels: 0 us -> 17.6 us
  matrix products: 13.7 us -> 0 us
    another operation x20 -> x0, other arithmetic: 105 us -> none  [the longest x4 34 us: rotation(): jax.scipy.linalg.cho_solve((right_factor, True), -2.0 * coupling.T)]
    all_to_all x6 -> x0, waiting for transfers between devices: 53.7 us -> none  [the longest x4 33.9 us: from_everyone(): lax.all_to_all(jnp.broadcast_to(value[None], (devices, *value.shape)), ax...]
    all_to_all x6 -> x0, starting transfers between devices: 33.6 us -> none  [the longest x4 25.5 us: from_everyone(): lax.all_to_all(jnp.broadcast_to(value[None], (devices, *value.shape)), ax...]
    ppermute x2 -> x18, starting transfers between devices: 3.73 us -> 35.3 us  [the longest x16 31.7 us: across(): return lax.ppermute(value, 'row', row_route(**kinds))]
    all_to_all x2 -> x0, blocking collectives: 25.9 us -> none  [from_everyone(): lax.all_to_all(jnp.broadcast_to(value[None], (devices, *value.shape)), ax...]
    ppermute x2 -> x18, waiting for transfers between devices: 4.66 us -> 22.5 us  [the longest x16 16.2 us: across(): return lax.ppermute(value, 'row', row_route(**kinds))]
    pallas_call x0 -> x4, Pallas kernels: none -> 17.6 us  [the longest x2 13.7 us: rotated(): pl.pallas_call(functools.partial(rotate_kernel, row_total), out_shape=(ja...]
    dot_general x14 -> x0, matrix products: 9.83 us -> none  [the longest x4 3.44 us: rotate(): jnp.dot(first_part, from_first, precision=highest)]
  transfers between devices with their start and end apart: 8 -> 18, of which waited for: 7 -> 15; matrix products, arithmetic and copies ran while one was open for 2% -> 0% of each run, Pallas kernels for 0% -> 0%
where the time goes in v1:
time: 80.6 us; the launch traced here: 80.3 us
  starting transfers between devices  35.3 us (44%)
  waiting for transfers between devices  22.5 us (28%)
  Pallas kernels  17.6 us (22%)
  local copies, waits for them, and re-layouts  2.61 us (3%)
  other arithmetic  1.59 us (2%)
    ppermute x16, starting transfers between devices, across(): return lax.ppermute(value, 'row', row_route(**kinds))  31.7 us
    ppermute x16, waiting for transfers between devices, across(): return lax.ppermute(value, 'row', row_route(**kinds))  16.2 us
    pallas_call x2, Pallas kernels, rotated(): pl.pallas_call(functools.partial(rotate_kernel, row_total), out_shape=(ja...  13.7 us
    ppermute x2, waiting for transfers between devices, from_behind(): lax.ppermute(block, 'col', [((i - distance) % devices, i) for i in range(...  6.29 us
    pallas_call x2, Pallas kernels, statistics(): pl.pallas_call(statistics_kernel, out_shape=(half, half), in_specs=[vmem,...  3.95 us
    ppermute x2, starting transfers between devices, from_behind(): lax.ppermute(block, 'col', [((i - distance) % devices, i) for i in range(...  3.58 us
    unnamed x12, local copies, waits for them, and re-layouts  2.61 us
  transfers between devices with their start and end apart: 18, of which 15 were waited for; matrix products, arithmetic and copies ran while one was open for 0% of the time, Pallas kernels for 0%

profile of v1, /device:TPU:1, one launch (start us, length us, event | category | flops | bytes accessed | tf_op | source)
XLA Modules:
  0.0 80.3 jit_solution(15330856183683224393)
XLA Ops:
  0.6 2.0 %statistics.2 = (f32[72,128]{1,0:T(8,128)}, f32[72,128]{1,0:T(8,128)}) custom-call(f32[512,128]{1,0:T(8,128)} %upper_ref.3, f32[512,128]{1,0:T(8,128)} %lower_ref.3), custom_call_target="tpu_custom_call" | custom-call | tf_op jit(solution)/shard_map/statistics/pallas_call | solution.py:74
  2.6 3.2 %collective-permute-start = (f32[72,128]{1,0:T(8,128)}, f32[72,128]{1,0:T(8,128)S(1)}, u32[]{:S(2)}, u32[]{:S(2)}) collective-permute-start(f32[72,128]{1,0:T(8,128)} %get-tuple-element.9), channel_id=1, source_target_pairs={{0,1},{1,0},{2,3},{3,2},{4,5},{5,4},{6,7},{7,6},{8,9},{9,8},{10,11... | collective-permute-start | bytes 110600 | tf_op jit(solution)/shard_map/ppermute | solution.py:32
  5.8 1.1 %collective-permute-done = f32[72,128]{1,0:T(8,128)S(1)} collective-permute-done((f32[72,128]{1,0:T(8,128)}, f32[72,128]{1,0:T(8,128)S(1)}, u32[]{:S(2)}, u32[]{:S(2)}) %collective-permute-start) | collective-permute-done | bytes 36896 | tf_op jit(solution)/shard_map/ppermute | solution.py:32
  6.9 0.8 add.42
  7.7 2.4 %collective-permute-start.3 = (f32[72,128]{1,0:T(8,128)S(1)}, f32[72,128]{1,0:T(8,128)S(1)}, u32[]{:S(2)}, u32[]{:S(2)}) collective-permute-start(f32[72,128]{1,0:T(8,128)S(1)} %add.42), channel_id=1, source_target_pairs={{0,6},{1,7},{2,4},{3,5},{4,2},{5,3},{6,0},{7,1},{8,14},{9,15},{10,... | collective-permute-start | bytes 110600 | tf_op jit(solution)/shard_map/ppermute | solution.py:32
  10.1 0.0 collective-permute-start.2
  10.1 1.8 %collective-permute-start.1 = (f32[72,128]{1,0:T(8,128)S(1)}, f32[72,128]{1,0:T(8,128)S(1)}, u32[]{:S(2)}, u32[]{:S(2)}) collective-permute-start(f32[72,128]{1,0:T(8,128)S(1)} %add.42), channel_id=1, source_target_pairs={{0,2},{1,3},{2,0},{3,1},{4,6},{5,7},{6,4},{7,5},{8,10},{9,11},{10,... | collective-permute-start | bytes 110600 | tf_op jit(solution)/shard_map/ppermute | solution.py:32
  11.9 1.1 %collective-permute-done.3 = f32[72,128]{1,0:T(8,128)S(1)} collective-permute-done((f32[72,128]{1,0:T(8,128)S(1)}, f32[72,128]{1,0:T(8,128)S(1)}, u32[]{:S(2)}, u32[]{:S(2)}) %collective-permute-start.3) | collective-permute-done | bytes 36896 | tf_op jit(solution)/shard_map/ppermute | solution.py:32
  12.9 0.3 collective-permute-done.2
  13.2 1.2 %collective-permute-done.1 = f32[72,128]{1,0:T(8,128)S(1)} collective-permute-done((f32[72,128]{1,0:T(8,128)S(1)}, f32[72,128]{1,0:T(8,128)S(1)}, u32[]{:S(2)}, u32[]{:S(2)}) %collective-permute-start.1) | collective-permute-done | bytes 36896 | tf_op jit(solution)/shard_map/ppermute | solution.py:32
  14.4 6.4 %collective-permute-start.6 = (f32[72,128]{1,0:T(8,128)S(1)}, f32[72,128]{1,0:T(8,128)S(1)}, u32[]{:S(2)}, u32[]{:S(2)}) collective-permute-start(f32[72,128]{1,0:T(8,128)S(1)} %add_add_fusion.3), channel_id=1, source_target_pairs={{0,20},{1,21},{2,22},{3,23},{4,16},{5,17},{6,18},{7,19},{8,28},{9,... | collective-permute-start | bytes 110600 | tf_op jit(solution)/shard_map/ppermute | solution.py:32
  20.8 0.3 collective-permute-start.5
  21.0 0.9 %collective-permute-start.4 = (f32[72,128]{1,0:T(8,128)S(1)}, f32[72,128]{1,0:T(8,128)S(1)}, u32[]{:S(2)}, u32[]{:S(2)}) collective-permute-start(f32[72,128]{1,0:T(8,128)S(1)} %add_add_fusion.3), channel_id=1, source_target_pairs={{0,8},{1,9},{2,10},{3,11},{4,12},{5,13},{6,14},{7,15},{8,0},{9,1},... | collective-permute-start | bytes 110600 | tf_op jit(solution)/shard_map/ppermute | solution.py:32
  22.0 0.2 collective-permute-done.6
  22.1 3.6 %collective-permute-done.5 = f32[72,128]{1,0:T(8,128)S(1)} collective-permute-done((f32[72,128]{1,0:T(8,128)S(1)}, f32[72,128]{1,0:T(8,128)S(1)}, u32[]{:S(2)}, u32[]{:S(2)}) %collective-permute-start.5) | collective-permute-done | bytes 36896 | tf_op jit(solution)/shard_map/ppermute | solution.py:32
  25.7 0.0 collective-permute-done.4
  25.7 0.0 copy-start.3
  25.7 3.6 %collective-permute-start.7 = (f32[72,128]{1,0:T(8,128)S(1)}, f32[72,128]{1,0:T(8,128)S(1)}, u32[]{:S(2)}, u32[]{:S(2)}) collective-permute-start(f32[72,128]{1,0:T(8,128)S(1)} %add_add_fusion.2.mine_ref), channel_id=1, source_target_pairs={{0,1},{1,0},{2,3},{3,2},{4,5},{5,4},{6,7},{7,6},{8,9},{9,8},{10,11... | collective-permute-start | bytes 110600 | tf_op jit(solution)/shard_map/ppermute | solution.py:32
  29.3 0.9 %collective-permute-done.7.other_ref = f32[72,128]{1,0:T(8,128)S(1)} collective-permute-done((f32[72,128]{1,0:T(8,128)S(1)}, f32[72,128]{1,0:T(8,128)S(1)}, u32[]{:S(2)}, u32[]{:S(2)}) %collective-permute-start.7) | collective-permute-done | bytes 36896 | tf_op jit(solution)/shard_map/ppermute | solution.py:32
  30.2 0.0 copy-done.3
  30.2 0.6 copy-done.5
  30.8 6.8 %rotate.2 = (f32[512,128]{1,0:T(8,128)}, f32[512,128]{1,0:T(8,128)}) custom-call(f32[72,128]{1,0:T(8,128)} %copy-done.3, f32[72,128]{1,0:T(8,128)} %copy-done.5, f32[512,128]{1,0:T(8,128)} %upper_ref.3, f32[512,128]{1,0:T(8,128)} %lower_ref.3), custom_call_target="tpu_custom_call" | custom-call | tf_op jit(solution)/shard_map/rotate/pallas_call | solution.py:137
  37.6 1.3 %collective-permute-start.8 = (f32[512,128]{1,0:T(8,128)}, f32[512,128]{1,0:T(8,128)S(1)}, u32[]{:S(2)}, u32[]{:S(2)}) collective-permute-start(f32[512,128]{1,0:T(8,128)} %get-tuple-element.10), channel_id=1, source_target_pairs={{224,0},{0,32},{32,64},{64,96},{96,128},{128,160},{160,192},{192,2... | collective-permute-start | bytes 786440 | tf_op jit(solution)/shard_map/ppermute | solution.py:149
  38.9 2.3 %collective-permute-start.9 = (f32[512,128]{1,0:T(8,128)}, f32[512,128]{1,0:T(8,128)S(1)}, u32[]{:S(2)}, u32[]{:S(2)}) collective-permute-start(f32[512,128]{1,0:T(8,128)} %get-tuple-element.11), channel_id=1, source_target_pairs={{32,0},{64,32},{96,64},{128,96},{160,128},{192,160},{224,192},{0,2... | collective-permute-start | bytes 786440 | tf_op jit(solution)/shard_map/ppermute | solution.py:149
  41.2 6.3 %collective-permute-done.8.upper_ref = f32[512,128]{1,0:T(8,128)S(1)} collective-permute-done((f32[512,128]{1,0:T(8,128)}, f32[512,128]{1,0:T(8,128)S(1)}, u32[]{:S(2)}, u32[]{:S(2)}) %collective-permute-start.8) | collective-permute-done | bytes 262176 | tf_op jit(solution)/shard_map/ppermute | solution.py:149
  47.5 0.0 collective-permute-done.9.lower_ref
  47.5 0.7 copy-done
  48.2 0.7 copy-done.1
  48.9 2.0 %statistics.3 = (f32[72,128]{1,0:T(8,128)}, f32[72,128]{1,0:T(8,128)}) custom-call(f32[512,128]{1,0:T(8,128)} %copy-done, f32[512,128]{1,0:T(8,128)} %copy-done.1), custom_call_target="tpu_custom_call" | custom-call | tf_op jit(solution)/shard_map/statistics/pallas_call | solution.py:74
  50.8 1.2 %collective-permute-start.10 = (f32[72,128]{1,0:T(8,128)}, f32[72,128]{1,0:T(8,128)S(1)}, u32[]{:S(2)}, u32[]{:S(2)}) collective-permute-start(f32[72,128]{1,0:T(8,128)} %get-tuple-element.13), channel_id=1, source_target_pairs={{0,1},{1,0},{2,3},{3,2},{4,5},{5,4},{6,7},{7,6},{8,9},{9,8},{10,11... | collective-permute-start | bytes 110600 | tf_op jit(solution)/shard_map/ppermute | solution.py:32
  52.0 1.1 %collective-permute-done.10 = f32[72,128]{1,0:T(8,128)S(1)} collective-permute-done((f32[72,128]{1,0:T(8,128)}, f32[72,128]{1,0:T(8,128)S(1)}, u32[]{:S(2)}, u32[]{:S(2)}) %collective-permute-start.10) | collective-permute-done | bytes 36896 | tf_op jit(solution)/shard_map/ppermute | solution.py:32
  53.1 0.8 add.49
  53.9 1.4 %collective-permute-start.13 = (f32[72,128]{1,0:T(8,128)S(1)}, f32[72,128]{1,0:T(8,128)S(1)}, u32[]{:S(2)}, u32[]{:S(2)}) collective-permute-start(f32[72,128]{1,0:T(8,128)S(1)} %add.49), channel_id=1, source_target_pairs={{0,6},{1,7},{2,4},{3,5},{4,2},{5,3},{6,0},{7,1},{8,14},{9,15},{10,... | collective-permute-start | bytes 110600 | tf_op jit(solution)/shard_map/ppermute | solution.py:32
  55.2 0.7 collective-permute-start.12
  56.0 2.0 %collective-permute-start.11 = (f32[72,128]{1,0:T(8,128)S(1)}, f32[72,128]{1,0:T(8,128)S(1)}, u32[]{:S(2)}, u32[]{:S(2)}) collective-permute-start(f32[72,128]{1,0:T(8,128)S(1)} %add.49), channel_id=1, source_target_pairs={{0,2},{1,3},{2,0},{3,1},{4,6},{5,7},{6,4},{7,5},{8,10},{9,11},{10,... | collective-permute-start | bytes 110600 | tf_op jit(solution)/shard_map/ppermute | solution.py:32
  58.0 1.1 %collective-permute-done.13 = f32[72,128]{1,0:T(8,128)S(1)} collective-permute-done((f32[72,128]{1,0:T(8,128)S(1)}, f32[72,128]{1,0:T(8,128)S(1)}, u32[]{:S(2)}, u32[]{:S(2)}) %collective-permute-start.13) | collective-permute-done | bytes 36896 | tf_op jit(solution)/shard_map/ppermute | solution.py:32
  59.1 0.0 collective-permute-done.12
  59.1 1.4 %collective-permute-done.11 = f32[72,128]{1,0:T(8,128)S(1)} collective-permute-done((f32[72,128]{1,0:T(8,128)S(1)}, f32[72,128]{1,0:T(8,128)S(1)}, u32[]{:S(2)}, u32[]{:S(2)}) %collective-permute-start.11) | collective-permute-done | bytes 36896 | tf_op jit(solution)/shard_map/ppermute | solution.py:32
  60.5 3.2 %collective-permute-start.16 = (f32[72,128]{1,0:T(8,128)S(1)}, f32[72,128]{1,0:T(8,128)S(1)}, u32[]{:S(2)}, u32[]{:S(2)}) collective-permute-start(f32[72,128]{1,0:T(8,128)S(1)} %add_add_fusion.1), channel_id=1, source_target_pairs={{0,20},{1,21},{2,22},{3,23},{4,16},{5,17},{6,18},{7,19},{8,28},{9,... | collective-permute-start | bytes 110600 | tf_op jit(solution)/shard_map/ppermute | solution.py:32
  63.7 0.9 %collective-permute-start.15 = (f32[72,128]{1,0:T(8,128)S(1)}, f32[72,128]{1,0:T(8,128)S(1)}, u32[]{:S(2)}, u32[]{:S(2)}) collective-permute-start(f32[72,128]{1,0:T(8,128)S(1)} %add_add_fusion.1), channel_id=1, source_target_pairs={{0,24},{1,25},{2,26},{3,27},{4,28},{5,29},{6,30},{7,31},{8,16},{9,... | collective-permute-start | bytes 110600 | tf_op jit(solution)/shard_map/ppermute | solution.py:32
  64.6 1.2 %collective-permute-start.14 = (f32[72,128]{1,0:T(8,128)S(1)}, f32[72,128]{1,0:T(8,128)S(1)}, u32[]{:S(2)}, u32[]{:S(2)}) collective-permute-start(f32[72,128]{1,0:T(8,128)S(1)} %add_add_fusion.1), channel_id=1, source_target_pairs={{0,8},{1,9},{2,10},{3,11},{4,12},{5,13},{6,14},{7,15},{8,0},{9,1},... | collective-permute-start | bytes 110600 | tf_op jit(solution)/shard_map/ppermute | solution.py:32
  65.8 0.6 collective-permute-done.16
  66.4 2.7 %collective-permute-done.15 = f32[72,128]{1,0:T(8,128)S(1)} collective-permute-done((f32[72,128]{1,0:T(8,128)S(1)}, f32[72,128]{1,0:T(8,128)S(1)}, u32[]{:S(2)}, u32[]{:S(2)}) %collective-permute-start.15) | collective-permute-done | bytes 36896 | tf_op jit(solution)/shard_map/ppermute | solution.py:32
  69.1 0.3 collective-permute-done.14
  69.4 2.6 %collective-permute-start.17 = (f32[72,128]{1,0:T(8,128)S(1)}, f32[72,128]{1,0:T(8,128)S(1)}, u32[]{:S(2)}, u32[]{:S(2)}) collective-permute-start(f32[72,128]{1,0:T(8,128)S(1)} %add_add_fusion.mine_ref), channel_id=1, source_target_pairs={{0,1},{1,0},{2,3},{3,2},{4,5},{5,4},{6,7},{7,6},{8,9},{9,8},{10,11... | collective-permute-start | bytes 110600 | tf_op jit(solution)/shard_map/ppermute | solution.py:32
  72.0 0.9 %collective-permute-done.17.other_ref = f32[72,128]{1,0:T(8,128)S(1)} collective-permute-done((f32[72,128]{1,0:T(8,128)S(1)}, f32[72,128]{1,0:T(8,128)S(1)}, u32[]{:S(2)}, u32[]{:S(2)}) %collective-permute-start.17) | collective-permute-done | bytes 36896 | tf_op jit(solution)/shard_map/ppermute | solution.py:32
  72.9 0.6 copy-done.4
  73.5 6.8 %rotate.3 = (f32[512,128]{1,0:T(8,128)}, f32[512,128]{1,0:T(8,128)}) custom-call(f32[72,128]{1,0:T(8,128)} %copy-done.2, f32[72,128]{1,0:T(8,128)} %copy-done.4, f32[512,128]{1,0:T(8,128)} %copy-done, f32[512,128]{1,0:T(8,128)} %copy-done.1), custom_call_target="tpu_custom_call" | custom-call | tf_op jit(solution)/shard_map/rotate/pallas_call | solution.py:137
  (10 shorter events, 0.1 us)
Async XLA Ops:
  2.6 4.3 %collective-permute-start = (f32[72,128]{1,0:T(8,128)}, f32[72,128]{1,0:T(8,128)S(1)}, u32[]{:S(2)}, u32[]{:S(2)}) collective-permute-start(f32[72,128]{1,0:T(8,128)} %get-tuple-element.9), channel_id=1, source_target_pairs={{0,1},{1,0},{2,3},{3,2},{4,5},{5,4},{6,7},{7,6},{8,9},{9,8},{10,11... | collective-permute-start | bytes 110600 | tf_op jit(solution)/shard_map/ppermute | solution.py:32
  7.7 5.2 %collective-permute-start.3 = (f32[72,128]{1,0:T(8,128)S(1)}, f32[72,128]{1,0:T(8,128)S(1)}, u32[]{:S(2)}, u32[]{:S(2)}) collective-permute-start(f32[72,128]{1,0:T(8,128)S(1)} %add.42), channel_id=1, source_target_pairs={{0,6},{1,7},{2,4},{3,5},{4,2},{5,3},{6,0},{7,1},{8,14},{9,15},{10,... | collective-permute-start | bytes 110600 | tf_op jit(solution)/shard_map/ppermute | solution.py:32
  10.1 3.1 %collective-permute-start.2 = (f32[72,128]{1,0:T(8,128)S(1)}, f32[72,128]{1,0:T(8,128)S(1)}, u32[]{:S(2)}, u32[]{:S(2)}) collective-permute-start(f32[72,128]{1,0:T(8,128)S(1)} %add.42), channel_id=1, source_target_pairs={{0,4},{1,5},{2,6},{3,7},{4,0},{5,1},{6,2},{7,3},{8,12},{9,13},{10,... | collective-permute-start | bytes 110600 | tf_op jit(solution)/shard_map/ppermute | solution.py:32
  10.1 4.3 %collective-permute-start.1 = (f32[72,128]{1,0:T(8,128)S(1)}, f32[72,128]{1,0:T(8,128)S(1)}, u32[]{:S(2)}, u32[]{:S(2)}) collective-permute-start(f32[72,128]{1,0:T(8,128)S(1)} %add.42), channel_id=1, source_target_pairs={{0,2},{1,3},{2,0},{3,1},{4,6},{5,7},{6,4},{7,5},{8,10},{9,11},{10,... | collective-permute-start | bytes 110600 | tf_op jit(solution)/shard_map/ppermute | solution.py:32
  14.4 7.7 %collective-permute-start.6 = (f32[72,128]{1,0:T(8,128)S(1)}, f32[72,128]{1,0:T(8,128)S(1)}, u32[]{:S(2)}, u32[]{:S(2)}) collective-permute-start(f32[72,128]{1,0:T(8,128)S(1)} %add_add_fusion.3), channel_id=1, source_target_pairs={{0,20},{1,21},{2,22},{3,23},{4,16},{5,17},{6,18},{7,19},{8,28},{9,... | collective-permute-start | bytes 110600 | tf_op jit(solution)/shard_map/ppermute | solution.py:32
  20.8 4.9 %collective-permute-start.5 = (f32[72,128]{1,0:T(8,128)S(1)}, f32[72,128]{1,0:T(8,128)S(1)}, u32[]{:S(2)}, u32[]{:S(2)}) collective-permute-start(f32[72,128]{1,0:T(8,128)S(1)} %add_add_fusion.3), channel_id=1, source_target_pairs={{0,24},{1,25},{2,26},{3,27},{4,28},{5,29},{6,30},{7,31},{8,16},{9,... | collective-permute-start | bytes 110600 | tf_op jit(solution)/shard_map/ppermute | solution.py:32
  21.0 4.7 %collective-permute-start.4 = (f32[72,128]{1,0:T(8,128)S(1)}, f32[72,128]{1,0:T(8,128)S(1)}, u32[]{:S(2)}, u32[]{:S(2)}) collective-permute-start(f32[72,128]{1,0:T(8,128)S(1)} %add_add_fusion.3), channel_id=1, source_target_pairs={{0,8},{1,9},{2,10},{3,11},{4,12},{5,13},{6,14},{7,15},{8,0},{9,1},... | collective-permute-start | bytes 110600 | tf_op jit(solution)/shard_map/ppermute | solution.py:32
  25.7 4.4 %copy-start.3 = (f32[72,128]{1,0:T(8,128)}, f32[72,128]{1,0:T(8,128)S(1)}, u32[]{:S(2)}) copy-start(f32[72,128]{1,0:T(8,128)S(1)} %add_add_fusion.2.mine_ref) | copy-start | bytes 110596
  25.7 4.4 %collective-permute-start.7 = (f32[72,128]{1,0:T(8,128)S(1)}, f32[72,128]{1,0:T(8,128)S(1)}, u32[]{:S(2)}, u32[]{:S(2)}) collective-permute-start(f32[72,128]{1,0:T(8,128)S(1)} %add_add_fusion.2.mine_ref), channel_id=1, source_target_pairs={{0,1},{1,0},{2,3},{3,2},{4,5},{5,4},{6,7},{7,6},{8,9},{9,8},{10,11... | collective-permute-start | bytes 110600 | tf_op jit(solution)/shard_map/ppermute | solution.py:32
  30.2 0.6 copy-start.5
  37.6 9.9 %collective-permute-start.8 = (f32[512,128]{1,0:T(8,128)}, f32[512,128]{1,0:T(8,128)S(1)}, u32[]{:S(2)}, u32[]{:S(2)}) collective-permute-start(f32[512,128]{1,0:T(8,128)} %get-tuple-element.10), channel_id=1, source_target_pairs={{224,0},{0,32},{32,64},{64,96},{96,128},{128,160},{160,192},{192,2... | collective-permute-start | bytes 786440 | tf_op jit(solution)/shard_map/ppermute | solution.py:149
  38.9 8.6 %collective-permute-start.9 = (f32[512,128]{1,0:T(8,128)}, f32[512,128]{1,0:T(8,128)S(1)}, u32[]{:S(2)}, u32[]{:S(2)}) collective-permute-start(f32[512,128]{1,0:T(8,128)} %get-tuple-element.11), channel_id=1, source_target_pairs={{32,0},{64,32},{96,64},{128,96},{160,128},{192,160},{224,192},{0,2... | collective-permute-start | bytes 786440 | tf_op jit(solution)/shard_map/ppermute | solution.py:149
  47.5 0.7 copy-start
  48.2 0.7 copy-start.1
  50.8 2.3 %collective-permute-start.10 = (f32[72,128]{1,0:T(8,128)}, f32[72,128]{1,0:T(8,128)S(1)}, u32[]{:S(2)}, u32[]{:S(2)}) collective-permute-start(f32[72,128]{1,0:T(8,128)} %get-tuple-element.13), channel_id=1, source_target_pairs={{0,1},{1,0},{2,3},{3,2},{4,5},{5,4},{6,7},{7,6},{8,9},{9,8},{10,11... | collective-permute-start | bytes 110600 | tf_op jit(solution)/shard_map/ppermute | solution.py:32
  53.9 5.2 %collective-permute-start.13 = (f32[72,128]{1,0:T(8,128)S(1)}, f32[72,128]{1,0:T(8,128)S(1)}, u32[]{:S(2)}, u32[]{:S(2)}) collective-permute-start(f32[72,128]{1,0:T(8,128)S(1)} %add.49), channel_id=1, source_target_pairs={{0,6},{1,7},{2,4},{3,5},{4,2},{5,3},{6,0},{7,1},{8,14},{9,15},{10,... | collective-permute-start | bytes 110600 | tf_op jit(solution)/shard_map/ppermute | solution.py:32
  55.2 3.8 %collective-permute-start.12 = (f32[72,128]{1,0:T(8,128)S(1)}, f32[72,128]{1,0:T(8,128)S(1)}, u32[]{:S(2)}, u32[]{:S(2)}) collective-permute-start(f32[72,128]{1,0:T(8,128)S(1)} %add.49), channel_id=1, source_target_pairs={{0,4},{1,5},{2,6},{3,7},{4,0},{5,1},{6,2},{7,3},{8,12},{9,13},{10,... | collective-permute-start | bytes 110600 | tf_op jit(solution)/shard_map/ppermute | solution.py:32
  56.0 4.5 %collective-permute-start.11 = (f32[72,128]{1,0:T(8,128)S(1)}, f32[72,128]{1,0:T(8,128)S(1)}, u32[]{:S(2)}, u32[]{:S(2)}) collective-permute-start(f32[72,128]{1,0:T(8,128)S(1)} %add.49), channel_id=1, source_target_pairs={{0,2},{1,3},{2,0},{3,1},{4,6},{5,7},{6,4},{7,5},{8,10},{9,11},{10,... | collective-permute-start | bytes 110600 | tf_op jit(solution)/shard_map/ppermute | solution.py:32
  60.5 5.9 %collective-permute-start.16 = (f32[72,128]{1,0:T(8,128)S(1)}, f32[72,128]{1,0:T(8,128)S(1)}, u32[]{:S(2)}, u32[]{:S(2)}) collective-permute-start(f32[72,128]{1,0:T(8,128)S(1)} %add_add_fusion.1), channel_id=1, source_target_pairs={{0,20},{1,21},{2,22},{3,23},{4,16},{5,17},{6,18},{7,19},{8,28},{9,... | collective-permute-start | bytes 110600 | tf_op jit(solution)/shard_map/ppermute | solution.py:32
  63.7 5.4 %collective-permute-start.15 = (f32[72,128]{1,0:T(8,128)S(1)}, f32[72,128]{1,0:T(8,128)S(1)}, u32[]{:S(2)}, u32[]{:S(2)}) collective-permute-start(f32[72,128]{1,0:T(8,128)S(1)} %add_add_fusion.1), channel_id=1, source_target_pairs={{0,24},{1,25},{2,26},{3,27},{4,28},{5,29},{6,30},{7,31},{8,16},{9,... | collective-permute-start | bytes 110600 | tf_op jit(solution)/shard_map/ppermute | solution.py:32
  64.6 4.8 %collective-permute-start.14 = (f32[72,128]{1,0:T(8,128)S(1)}, f32[72,128]{1,0:T(8,128)S(1)}, u32[]{:S(2)}, u32[]{:S(2)}) collective-permute-start(f32[72,128]{1,0:T(8,128)S(1)} %add_add_fusion.1), channel_id=1, source_target_pairs={{0,8},{1,9},{2,10},{3,11},{4,12},{5,13},{6,14},{7,15},{8,0},{9,1},... | collective-permute-start | bytes 110600 | tf_op jit(solution)/shard_map/ppermute | solution.py:32
  69.4 3.4 %copy-start.2 = (f32[72,128]{1,0:T(8,128)}, f32[72,128]{1,0:T(8,128)S(1)}, u32[]{:S(2)}) copy-start(f32[72,128]{1,0:T(8,128)S(1)} %add_add_fusion.mine_ref) | copy-start | bytes 110596
  69.4 3.4 %collective-permute-start.17 = (f32[72,128]{1,0:T(8,128)S(1)}, f32[72,128]{1,0:T(8,128)S(1)}, u32[]{:S(2)}, u32[]{:S(2)}) collective-permute-start(f32[72,128]{1,0:T(8,128)S(1)} %add_add_fusion.mine_ref), channel_id=1, source_target_pairs={{0,1},{1,0},{2,3},{3,2},{4,5},{5,4},{6,7},{7,6},{8,9},{9,8},{10,11... | collective-permute-start | bytes 110600 | tf_op jit(solution)/shard_map/ppermute | solution.py:32
  72.9 0.6 copy-start.4

commit v2 on v1

v2 whole, which is shorter than its diff:
```python
import functools

import jax
import jax.numpy as jnp
from jax import lax
from jax.experimental import pallas as pl
from jax.experimental.pallas import tpu as pltpu
from jax.sharding import PartitionSpec as P

ROUNDS = 2
FIRST_LIMIT = 56_400_000
HALF_ROWS = 72
TOLERANCE = 1e-7

Z_PAIR = {0: 1, 2: 3, 4: 5, 6: 7}
Z_FAR = ({0: 2, 1: 3, 4: 6, 5: 7}, {0: 6, 1: 7, 2: 4, 3: 5}, {0: 5, 1: 4, 2: 7, 3: 6})


def both_ways(pairs):
    return {**pairs, **{b: a for a, b in pairs.items()}}


def row_route(z_map=None, flip_x=False, flip_core=False):
    route = []
    for i in range(32):
        z, x, core = i // 4, i // 2 % 2, i % 2
        z = both_ways(z_map)[z] if z_map else z
        route.append((i, z * 4 + (x ^ flip_x) * 2 + (core ^ flip_core)))
    return route


def across(value, **kinds):
    return lax.ppermute(value, "row", row_route(**kinds))


def summed_over_chips(value):
    near = [across(value, flip_x=True), across(value, z_map=Z_PAIR), across(value, z_map=Z_PAIR, flip_x=True)]
    value = (value + near[0]) + (near[1] + near[2])
    far = [across(value, z_map=pairs) for pairs in Z_FAR]
    return (value + far[0]) + (far[1] + far[2])


def split(value):
    high = value.astype(jnp.bfloat16)
    return high, (value - high.astype(jnp.float32)).astype(jnp.bfloat16)


def contract(a, b, dims):
    (ah, al), (bh, bl) = a, b
    dot = functools.partial(lax.dot_general, dimension_numbers=(dims, ((), ())), preferred_element_type=jnp.float32)
    return dot(ah, bh) + (dot(al, bh) + dot(ah, bl))


def exact_dot(a, b, dims=((1,), (0,))):
    return lax.dot_general(
        a, b, dimension_numbers=(dims, ((), ())), precision=lax.Precision.HIGHEST, preferred_element_type=jnp.float32
    )


def write_statistics(upper, lower, keep_ref, send_ref):
    core = lax.axis_index("row") % 2
    gram = contract(split(upper), split(lower), ((0,), (0,)))
    sums = [jnp.sum((v * v).reshape(-1, 8, v.shape[1]), axis=0) for v in (upper, lower)]
    mine = core == 0
    keep_ref[:64] = jnp.where(mine, gram[:64], gram[64:])
    send_ref[:64] = jnp.where(mine, gram[64:], gram[:64])
    keep_ref[64:] = jnp.where(mine, sums[0], sums[1])
    send_ref[64:] = jnp.where(mine, sums[1], sums[0])


VMEM = pl.BlockSpec(memory_space=pltpu.VMEM)
HBM = pl.BlockSpec(memory_space=pltpu.HBM)
PARAMS = pltpu.CompilerParams(vmem_limit_bytes=8 << 20)
PIECES = 4


def pieces_of(rows):
    return [pl.ds(i * (rows // PIECES), rows // PIECES) for i in range(PIECES)]


def halves(width):
    return (jax.ShapeDtypeStruct((HALF_ROWS, width), jnp.float32),) * 2


def first_kernel(upper_hbm, lower_hbm, keep_ref, send_ref, upper_ref, lower_ref, sems):
    copies = [
        pltpu.make_async_copy(source.at[rows], target.at[rows], sems.at[i, j])
        for j, rows in enumerate(pieces_of(upper_hbm.shape[0]))
        for i, (source, target) in enumerate(((upper_hbm, upper_ref), (lower_hbm, lower_ref)))
    ]
    for copy in copies:
        copy.start()
    for copy in copies:
        copy.wait()
    write_statistics(upper_ref[...], lower_ref[...], keep_ref, send_ref)


def first_statistics(upper, lower):
    return pl.pallas_call(
        first_kernel,
        out_shape=halves(upper.shape[1]),
        in_specs=[HBM, HBM],
        out_specs=(VMEM, VMEM),
        scratch_shapes=[pltpu.VMEM(upper.shape, jnp.float32)] * 2 + [pltpu.SemaphoreType.DMA((2, PIECES))],
        compiler_params=pltpu.CompilerParams(vmem_limit_bytes=FIRST_LIMIT),
        name="first_statistics",
    )(upper, lower)


def statistics_kernel(upper_ref, lower_ref, keep_ref, send_ref):
    write_statistics(upper_ref[...], lower_ref[...], keep_ref, send_ref)


def statistics(upper, lower):
    return pl.pallas_call(
        statistics_kernel,
        out_shape=halves(upper.shape[1]),
        in_specs=[VMEM, VMEM],
        out_specs=(VMEM, VMEM),
        compiler_params=PARAMS,
        name="statistics",
    )(upper, lower)


def coupling_of(mine, other, row_total):
    core = lax.axis_index("row") % 2
    first = jnp.where(core == 0, mine, other)
    second = jnp.where(core == 0, other, mine)
    width = mine.shape[1]
    scale = 1.0 / row_total
    cross_gram = jnp.concatenate([first[:64], second[:64]], axis=0) * scale
    upper_norms = jnp.sum(first[64:], axis=0, keepdims=True) * scale
    lower_norms = jnp.sum(second[64:], axis=0, keepdims=True) * scale
    upper_norms = jnp.broadcast_to(upper_norms, (width, width)).T
    gap = upper_norms - lower_norms
    both = upper_norms + lower_norms
    return -cross_gram * gap / (2.0 * gap * gap + 0.5 * both * both + 1e-05)


def solved(coupling, residual_ref, result_ref):
    width = coupling.shape[0]
    identity = (
        lax.broadcasted_iota(jnp.int32, (width, width), 0) == lax.broadcasted_iota(jnp.int32, (width, width), 1)
    ).astype(jnp.float32)
    outer = exact_dot(coupling, coupling, ((1,), (1,)))
    size = jnp.sqrt(jnp.sum(jnp.sum(outer * outer, axis=0, keepdims=True), axis=1, keepdims=True))
    alpha = 2.0 / (2.0 + size)
    bound = jnp.sum(size / (2.0 + size))
    start = (1.0 - alpha) * identity - alpha * outer

    def factor(bound):
        residual = residual_ref[...]
        result = result_ref[...]
        result_ref[...] = result + exact_dot(residual, result)
        residual_ref[...] = exact_dot(residual, residual)
        return bound * bound

    def series(right):
        residual_ref[...] = start
        result_ref[...] = right
        lax.while_loop(lambda bound: bound > TOLERANCE, factor, bound)

    series((2.0 * alpha) * coupling)

    @pl.when(bound > 0.5)
    def _():
        for _ in range(2):
            value = result_ref[...]
            series(alpha * ((2.0 * coupling - value) - exact_dot(outer, value)))
            result_ref[...] += value

    return result_ref[...]


def change_of(mine, other, row_total, residual_ref, result_ref):
    coupling = coupling_of(mine, other, row_total)
    to_lower = solved(coupling, residual_ref, result_ref)
    upper_loss = exact_dot(coupling, to_lower, ((1,), (1,)))
    lower_loss = exact_dot(coupling, to_lower, ((0,), (0,)))
    return split(
        jnp.concatenate(
            [
                jnp.concatenate([-upper_loss, to_lower], axis=1),
                jnp.concatenate([-to_lower.T, -lower_loss], axis=1),
            ],
            axis=0,
        )
    )


def apply(upper, lower, change):
    width = upper.shape[1]
    moved = contract(split(jnp.concatenate([upper, lower], axis=1)), change, ((1,), (0,)))
    return upper + moved[:, :width], lower + moved[:, width:]


def rotate_kernel(row_total, mine_ref, other_ref, upper_ref, lower_ref, new_upper_ref, new_lower_ref, residual_ref, result_ref):
    change = change_of(mine_ref[...], other_ref[...], row_total, residual_ref, result_ref)
    new_upper_ref[...], new_lower_ref[...] = apply(upper_ref[...], lower_ref[...], change)


def last_kernel(row_total, mine_ref, other_ref, upper_ref, lower_ref, upper_hbm, lower_hbm, residual_ref, result_ref,
                new_upper_ref, new_lower_ref, sems):
    change = change_of(mine_ref[...], other_ref[...], row_total, residual_ref, result_ref)
    copies = []
    for j, rows in enumerate(pieces_of(upper_ref.shape[0])):
        new_upper_ref[rows], new_lower_ref[rows] = apply(upper_ref[rows], lower_ref[rows], change)
        for i, (source, target) in enumerate(((new_upper_ref, upper_hbm), (new_lower_ref, lower_hbm))):
            copies.append(pltpu.make_async_copy(source.at[rows], target.at[rows], sems.at[i, j]))
            copies[-1].start()
    for copy in copies:
        copy.wait()


def rotated(mine, other, upper, lower, row_total, last):
    square = pltpu.VMEM((upper.shape[1],) * 2, jnp.float32)
    scratch = [square, square]
    if last:
        scratch += [pltpu.VMEM(upper.shape, jnp.float32)] * 2 + [pltpu.SemaphoreType.DMA((2, PIECES))]
    return pl.pallas_call(
        functools.partial(last_kernel if last else rotate_kernel, row_total),
        out_shape=(jax.ShapeDtypeStruct(upper.shape, jnp.float32),) * 2,
        in_specs=[VMEM] * 4,
        out_specs=(HBM, HBM) if last else (VMEM, VMEM),
        scratch_shapes=scratch,
        compiler_params=PARAMS,
        name="rotate_last" if last else "rotate",
    )(mine, other, upper, lower)


def from_behind(block, distance):
    devices = lax.axis_size("col")
    return lax.ppermute(block, "col", [((i - distance) % devices, i) for i in range(devices)])


def shards(upper, lower):
    row_total = float(upper.shape[0] * lax.axis_size("row"))
    for round_index in range(ROUNDS):
        keep, send = statistics(upper, lower) if round_index else first_statistics(upper, lower)
        mine = summed_over_chips(keep + across(send, flip_core=True))
        other = across(mine, flip_core=True)
        last = round_index + 1 == ROUNDS
        upper, lower = rotated(mine, other, upper, lower, row_total, last)
        if not last:
            upper, lower = from_behind(upper, 1), from_behind(lower, -1)
    return upper, lower


def solution(mesh):
    placed = (P("row", "col"), P("row", "col"))
    return jax.shard_map(shards, mesh=mesh, in_specs=placed, out_specs=placed, check_vma=False)
```

time: 80.6 us -> 76.4 us (0.948)
  local copies, waits for them, and re-layouts: 2.61 us -> 0.01 us
  other arithmetic: 1.59 us -> 0.05 us
  waiting for transfers between devices: 22.5 us -> 21.4 us
    unnamed x12 -> x4, local copies, waits for them, and re-layouts: 2.61 us -> 0.01 us
    add x2, other arithmetic: 1.55 us -> 0.01 us  [shards(): mine = summed_over_chips(keep + across(send, flip_core=True))]
    ppermute x16, waiting for transfers between devices: 16.2 us -> 15.3 us  [across(): return lax.ppermute(value, 'row', row_route(**kinds))]
where the time goes in v2:
time: 76.4 us; the launch traced here: 76 us
  starting transfers between devices  35.3 us (46%)
  waiting for transfers between devices  21.4 us (28%)
  Pallas kernels  18.4 us (24%)
    ppermute x16, starting transfers between devices, across(): return lax.ppermute(value, 'row', row_route(**kinds))  31.7 us
    pallas_call x2, Pallas kernels, rotated(): pl.pallas_call(functools.partial(last_kernel if last else rotate_kernel,...  16.6 us
    ppermute x16, waiting for transfers between devices, across(): return lax.ppermute(value, 'row', row_route(**kinds))  15.3 us
    ppermute x2, waiting for transfers between devices, from_behind(): lax.ppermute(block, 'col', [((i - distance) % devices, i) for i in range(...  6.07 us
    ppermute x2, starting transfers between devices, from_behind(): lax.ppermute(block, 'col', [((i - distance) % devices, i) for i in range(...  3.65 us
  transfers between devices with their start and end apart: 18, of which 15 were waited for; matrix products, arithmetic and copies ran while one was open for 0% of the time, Pallas kernels for 0%

profile of v2, /device:TPU:1, one launch (start us, length us, event | category | flops | bytes accessed | tf_op | source)
XLA Modules:
  0.0 76.0 jit_solution(6174254322685753824)
XLA Ops:
  0.6 0.0 copy-start.1
  0.6 1.5 %first_statistics.1 = (f32[72,128]{1,0:T(8,128)S(1)}, f32[72,128]{1,0:T(8,128)S(1)}) custom-call(f32[512,128]{1,0:T(8,128)} %upper_ref.1, f32[512,128]{1,0:T(8,128)} %lower_ref.1), custom_call_target="tpu_custom_call" | custom-call | tf_op jit(solution)/shard_map/first_statistics/pallas_call | solution.py:99
  2.1 0.0 copy-start
  2.1 3.3 %collective-permute-start = (f32[72,128]{1,0:T(8,128)S(1)}, f32[72,128]{1,0:T(8,128)S(1)}, u32[]{:S(2)}, u32[]{:S(2)}) collective-permute-start(f32[72,128]{1,0:T(8,128)S(1)} %get-tuple-element.9), channel_id=1, source_target_pairs={{0,1},{1,0},{2,3},{3,2},{4,5},{5,4},{6,7},{7,6},{8,9},{9,8},{10,11... | collective-permute-start | bytes 110600 | tf_op jit(solution)/shard_map/ppermute | solution.py:33
  5.5 0.9 %collective-permute-done = f32[72,128]{1,0:T(8,128)S(1)} collective-permute-done((f32[72,128]{1,0:T(8,128)S(1)}, f32[72,128]{1,0:T(8,128)S(1)}, u32[]{:S(2)}, u32[]{:S(2)}) %collective-permute-start) | collective-permute-done | bytes 36896 | tf_op jit(solution)/shard_map/ppermute | solution.py:33
  6.3 2.4 %collective-permute-start.3 = (f32[72,128]{1,0:T(8,128)S(1)}, f32[72,128]{1,0:T(8,128)S(1)}, u32[]{:S(2)}, u32[]{:S(2)}) collective-permute-start(f32[72,128]{1,0:T(8,128)S(1)} %add.42), channel_id=1, source_target_pairs={{0,6},{1,7},{2,4},{3,5},{4,2},{5,3},{6,0},{7,1},{8,14},{9,15},{10,... | collective-permute-start | bytes 110600 | tf_op jit(solution)/shard_map/ppermute | solution.py:33
  8.7 0.0 collective-permute-start.2
  8.7 1.8 %collective-permute-start.1 = (f32[72,128]{1,0:T(8,128)S(1)}, f32[72,128]{1,0:T(8,128)S(1)}, u32[]{:S(2)}, u32[]{:S(2)}) collective-permute-start(f32[72,128]{1,0:T(8,128)S(1)} %add.42), channel_id=1, source_target_pairs={{0,2},{1,3},{2,0},{3,1},{4,6},{5,7},{6,4},{7,5},{8,10},{9,11},{10,... | collective-permute-start | bytes 110600 | tf_op jit(solution)/shard_map/ppermute | solution.py:33
  10.5 1.1 %collective-permute-done.3 = f32[72,128]{1,0:T(8,128)S(1)} collective-permute-done((f32[72,128]{1,0:T(8,128)S(1)}, f32[72,128]{1,0:T(8,128)S(1)}, u32[]{:S(2)}, u32[]{:S(2)}) %collective-permute-start.3) | collective-permute-done | bytes 36896 | tf_op jit(solution)/shard_map/ppermute | solution.py:33
  11.6 0.3 collective-permute-done.2
  11.8 1.2 %collective-permute-done.1 = f32[72,128]{1,0:T(8,128)S(1)} collective-permute-done((f32[72,128]{1,0:T(8,128)S(1)}, f32[72,128]{1,0:T(8,128)S(1)}, u32[]{:S(2)}, u32[]{:S(2)}) %collective-permute-start.1) | collective-permute-done | bytes 36896 | tf_op jit(solution)/shard_map/ppermute | solution.py:33
  13.0 6.4 %collective-permute-start.6 = (f32[72,128]{1,0:T(8,128)S(1)}, f32[72,128]{1,0:T(8,128)S(1)}, u32[]{:S(2)}, u32[]{:S(2)}) collective-permute-start(f32[72,128]{1,0:T(8,128)S(1)} %add_add_fusion.3), channel_id=1, source_target_pairs={{0,20},{1,21},{2,22},{3,23},{4,16},{5,17},{6,18},{7,19},{8,28},{9,... | collective-permute-start | bytes 110600 | tf_op jit(solution)/shard_map/ppermute | solution.py:33
  19.4 0.3 collective-permute-start.5
  19.7 0.9 %collective-permute-start.4 = (f32[72,128]{1,0:T(8,128)S(1)}, f32[72,128]{1,0:T(8,128)S(1)}, u32[]{:S(2)}, u32[]{:S(2)}) collective-permute-start(f32[72,128]{1,0:T(8,128)S(1)} %add_add_fusion.3), channel_id=1, source_target_pairs={{0,8},{1,9},{2,10},{3,11},{4,12},{5,13},{6,14},{7,15},{8,0},{9,1},... | collective-permute-start | bytes 110600 | tf_op jit(solution)/shard_map/ppermute | solution.py:33
  20.6 0.2 collective-permute-done.6
  20.8 3.6 %collective-permute-done.5 = f32[72,128]{1,0:T(8,128)S(1)} collective-permute-done((f32[72,128]{1,0:T(8,128)S(1)}, f32[72,128]{1,0:T(8,128)S(1)}, u32[]{:S(2)}, u32[]{:S(2)}) %collective-permute-start.5) | collective-permute-done | bytes 36896 | tf_op jit(solution)/shard_map/ppermute | solution.py:33
  24.3 0.0 collective-permute-done.4
  24.4 3.6 %collective-permute-start.7 = (f32[72,128]{1,0:T(8,128)S(1)}, f32[72,128]{1,0:T(8,128)S(1)}, u32[]{:S(2)}, u32[]{:S(2)}) collective-permute-start(f32[72,128]{1,0:T(8,128)S(1)} %add_add_fusion.2.mine_ref), channel_id=1, source_target_pairs={{0,1},{1,0},{2,3},{3,2},{4,5},{5,4},{6,7},{7,6},{8,9},{9,8},{10,11... | collective-permute-start | bytes 110600 | tf_op jit(solution)/shard_map/ppermute | solution.py:33
  27.9 0.9 %collective-permute-done.7.other_ref = f32[72,128]{1,0:T(8,128)S(1)} collective-permute-done((f32[72,128]{1,0:T(8,128)S(1)}, f32[72,128]{1,0:T(8,128)S(1)}, u32[]{:S(2)}, u32[]{:S(2)}) %collective-permute-start.7) | collective-permute-done | bytes 36896 | tf_op jit(solution)/shard_map/ppermute | solution.py:33
  28.8 0.0 copy-done.1
  28.8 0.0 copy-done
  28.8 8.0 %rotate.1 = (f32[512,128]{1,0:T(8,128)S(1)}, f32[512,128]{1,0:T(8,128)S(1)}) custom-call(f32[72,128]{1,0:T(8,128)S(1)} %add_add_fusion.2.mine_ref, f32[72,128]{1,0:T(8,128)S(1)} %collective-permute-done.7.other_ref, f32[512,128]{1,0:T(8,128)S(1)} %copy-done, f32[512,128]{1,0:T(8,128)S(1)} %copy-done.1), custom_call_target="tpu_custom_call" | custom-call | tf_op jit(solution)/shard_map/rotate/pallas_call | solution.py:220
  36.8 0.6 collective-permute-start.8
  37.4 3.1 %collective-permute-start.9 = (f32[512,128]{1,0:T(8,128)S(1)}, f32[512,128]{1,0:T(8,128)S(1)}, u32[]{:S(2)}, u32[]{:S(2)}) collective-permute-start(f32[512,128]{1,0:T(8,128)S(1)} %get-tuple-element.11), channel_id=1, source_target_pairs={{32,0},{64,32},{96,64},{128,96},{160,128},{192,160},{224,192},{0,2... | collective-permute-start | bytes 786440 | tf_op jit(solution)/shard_map/ppermute | solution.py:233
  40.4 6.1 %collective-permute-done.8.upper_ref = f32[512,128]{1,0:T(8,128)S(1)} collective-permute-done((f32[512,128]{1,0:T(8,128)S(1)}, f32[512,128]{1,0:T(8,128)S(1)}, u32[]{:S(2)}, u32[]{:S(2)}) %collective-permute-start.8) | collective-permute-done | bytes 262176 | tf_op jit(solution)/shard_map/ppermute | solution.py:233
  46.5 0.0 collective-permute-done.9.lower_ref
  46.5 0.3 statistics.1
  46.8 1.3 %collective-permute-start.10 = (f32[72,128]{1,0:T(8,128)S(1)}, f32[72,128]{1,0:T(8,128)S(1)}, u32[]{:S(2)}, u32[]{:S(2)}) collective-permute-start(f32[72,128]{1,0:T(8,128)S(1)} %get-tuple-element.13), channel_id=1, source_target_pairs={{0,1},{1,0},{2,3},{3,2},{4,5},{5,4},{6,7},{7,6},{8,9},{9,8},{10,11... | collective-permute-start | bytes 110600 | tf_op jit(solution)/shard_map/ppermute | solution.py:33
  48.1 0.9 %collective-permute-done.10 = f32[72,128]{1,0:T(8,128)S(1)} collective-permute-done((f32[72,128]{1,0:T(8,128)S(1)}, f32[72,128]{1,0:T(8,128)S(1)}, u32[]{:S(2)}, u32[]{:S(2)}) %collective-permute-start.10) | collective-permute-done | bytes 36896 | tf_op jit(solution)/shard_map/ppermute | solution.py:33
  49.0 0.7 collective-permute-start.13
  49.6 0.7 collective-permute-start.12
  50.4 2.7 %collective-permute-start.11 = (f32[72,128]{1,0:T(8,128)S(1)}, f32[72,128]{1,0:T(8,128)S(1)}, u32[]{:S(2)}, u32[]{:S(2)}) collective-permute-start(f32[72,128]{1,0:T(8,128)S(1)} %add.49), channel_id=1, source_target_pairs={{0,2},{1,3},{2,0},{3,1},{4,6},{5,7},{6,4},{7,5},{8,10},{9,11},{10,... | collective-permute-start | bytes 110600 | tf_op jit(solution)/shard_map/ppermute | solution.py:33
  53.1 1.1 %collective-permute-done.13 = f32[72,128]{1,0:T(8,128)S(1)} collective-permute-done((f32[72,128]{1,0:T(8,128)S(1)}, f32[72,128]{1,0:T(8,128)S(1)}, u32[]{:S(2)}, u32[]{:S(2)}) %collective-permute-start.13) | collective-permute-done | bytes 36896 | tf_op jit(solution)/shard_map/ppermute | solution.py:33
  54.2 0.0 collective-permute-done.12
  54.2 0.9 %collective-permute-done.11 = f32[72,128]{1,0:T(8,128)S(1)} collective-permute-done((f32[72,128]{1,0:T(8,128)S(1)}, f32[72,128]{1,0:T(8,128)S(1)}, u32[]{:S(2)}, u32[]{:S(2)}) %collective-permute-start.11) | collective-permute-done | bytes 36896 | tf_op jit(solution)/shard_map/ppermute | solution.py:33
  55.1 3.2 %collective-permute-start.16 = (f32[72,128]{1,0:T(8,128)S(1)}, f32[72,128]{1,0:T(8,128)S(1)}, u32[]{:S(2)}, u32[]{:S(2)}) collective-permute-start(f32[72,128]{1,0:T(8,128)S(1)} %add_add_fusion.1), channel_id=1, source_target_pairs={{0,20},{1,21},{2,22},{3,23},{4,16},{5,17},{6,18},{7,19},{8,28},{9,... | collective-permute-start | bytes 110600 | tf_op jit(solution)/shard_map/ppermute | solution.py:33
  58.3 0.9 %collective-permute-start.15 = (f32[72,128]{1,0:T(8,128)S(1)}, f32[72,128]{1,0:T(8,128)S(1)}, u32[]{:S(2)}, u32[]{:S(2)}) collective-permute-start(f32[72,128]{1,0:T(8,128)S(1)} %add_add_fusion.1), channel_id=1, source_target_pairs={{0,24},{1,25},{2,26},{3,27},{4,28},{5,29},{6,30},{7,31},{8,16},{9,... | collective-permute-start | bytes 110600 | tf_op jit(solution)/shard_map/ppermute | solution.py:33
  59.2 1.2 %collective-permute-start.14 = (f32[72,128]{1,0:T(8,128)S(1)}, f32[72,128]{1,0:T(8,128)S(1)}, u32[]{:S(2)}, u32[]{:S(2)}) collective-permute-start(f32[72,128]{1,0:T(8,128)S(1)} %add_add_fusion.1), channel_id=1, source_target_pairs={{0,8},{1,9},{2,10},{3,11},{4,12},{5,13},{6,14},{7,15},{8,0},{9,1},... | collective-permute-start | bytes 110600 | tf_op jit(solution)/shard_map/ppermute | solution.py:33
  60.4 0.7 collective-permute-done.16
  61.0 2.7 %collective-permute-done.15 = f32[72,128]{1,0:T(8,128)S(1)} collective-permute-done((f32[72,128]{1,0:T(8,128)S(1)}, f32[72,128]{1,0:T(8,128)S(1)}, u32[]{:S(2)}, u32[]{:S(2)}) %collective-permute-start.15) | collective-permute-done | bytes 36896 | tf_op jit(solution)/shard_map/ppermute | solution.py:33
  63.7 0.2 collective-permute-done.14
  64.0 2.4 %collective-permute-start.17 = (f32[72,128]{1,0:T(8,128)S(1)}, f32[72,128]{1,0:T(8,128)S(1)}, u32[]{:S(2)}, u32[]{:S(2)}) collective-permute-start(f32[72,128]{1,0:T(8,128)S(1)} %add_add_fusion.mine_ref), channel_id=1, source_target_pairs={{0,1},{1,0},{2,3},{3,2},{4,5},{5,4},{6,7},{7,6},{8,9},{9,8},{10,11... | collective-permute-start | bytes 110600 | tf_op jit(solution)/shard_map/ppermute | solution.py:33
  66.4 0.9 %collective-permute-done.17.other_ref = f32[72,128]{1,0:T(8,128)S(1)} collective-permute-done((f32[72,128]{1,0:T(8,128)S(1)}, f32[72,128]{1,0:T(8,128)S(1)}, u32[]{:S(2)}, u32[]{:S(2)}) %collective-permute-start.17) | collective-permute-done | bytes 36896 | tf_op jit(solution)/shard_map/ppermute | solution.py:33
  67.3 8.7 %rotate_last.1 = (f32[512,128]{1,0:T(8,128)}, f32[512,128]{1,0:T(8,128)}) custom-call(f32[72,128]{1,0:T(8,128)S(1)} %add_add_fusion.mine_ref, f32[72,128]{1,0:T(8,128)S(1)} %collective-permute-done.17.other_ref, f32[512,128]{1,0:T(8,128)S(1)} %collective-permute-done.8.upper_ref, f32[512,128]{1,0:T(8,128)S(1)} %collective-permute-done.9.lower_ref), custom_call_target="tpu_custom_call" | custom-call | tf_op jit(solution)/shard_map/rotate_last/pallas_call | solution.py:220
  (6 shorter events, 0.1 us)
Async XLA Ops:
  0.6 28.2 %copy-start.1 = (f32[512,128]{1,0:T(8,128)S(1)}, f32[512,128]{1,0:T(8,128)}, u32[]{:S(2)}) copy-start(f32[512,128]{1,0:T(8,128)} %lower_ref.1) | copy-start | bytes 786436
  2.1 26.7 %copy-start = (f32[512,128]{1,0:T(8,128)S(1)}, f32[512,128]{1,0:T(8,128)}, u32[]{:S(2)}) copy-start(f32[512,128]{1,0:T(8,128)} %upper_ref.1) | copy-start | bytes 786436
  2.1 4.2 %collective-permute-start = (f32[72,128]{1,0:T(8,128)S(1)}, f32[72,128]{1,0:T(8,128)S(1)}, u32[]{:S(2)}, u32[]{:S(2)}) collective-permute-start(f32[72,128]{1,0:T(8,128)S(1)} %get-tuple-element.9), channel_id=1, source_target_pairs={{0,1},{1,0},{2,3},{3,2},{4,5},{5,4},{6,7},{7,6},{8,9},{9,8},{10,11... | collective-permute-start | bytes 110600 | tf_op jit(solution)/shard_map/ppermute | solution.py:33
  6.3 5.2 %collective-permute-start.3 = (f32[72,128]{1,0:T(8,128)S(1)}, f32[72,128]{1,0:T(8,128)S(1)}, u32[]{:S(2)}, u32[]{:S(2)}) collective-permute-start(f32[72,128]{1,0:T(8,128)S(1)} %add.42), channel_id=1, source_target_pairs={{0,6},{1,7},{2,4},{3,5},{4,2},{5,3},{6,0},{7,1},{8,14},{9,15},{10,... | collective-permute-start | bytes 110600 | tf_op jit(solution)/shard_map/ppermute | solution.py:33
  8.7 3.1 %collective-permute-start.2 = (f32[72,128]{1,0:T(8,128)S(1)}, f32[72,128]{1,0:T(8,128)S(1)}, u32[]{:S(2)}, u32[]{:S(2)}) collective-permute-start(f32[72,128]{1,0:T(8,128)S(1)} %add.42), channel_id=1, source_target_pairs={{0,4},{1,5},{2,6},{3,7},{4,0},{5,1},{6,2},{7,3},{8,12},{9,13},{10,... | collective-permute-start | bytes 110600 | tf_op jit(solution)/shard_map/ppermute | solution.py:33
  8.7 4.3 %collective-permute-start.1 = (f32[72,128]{1,0:T(8,128)S(1)}, f32[72,128]{1,0:T(8,128)S(1)}, u32[]{:S(2)}, u32[]{:S(2)}) collective-permute-start(f32[72,128]{1,0:T(8,128)S(1)} %add.42), channel_id=1, source_target_pairs={{0,2},{1,3},{2,0},{3,1},{4,6},{5,7},{6,4},{7,5},{8,10},{9,11},{10,... | collective-permute-start | bytes 110600 | tf_op jit(solution)/shard_map/ppermute | solution.py:33
  13.0 7.7 %collective-permute-start.6 = (f32[72,128]{1,0:T(8,128)S(1)}, f32[72,128]{1,0:T(8,128)S(1)}, u32[]{:S(2)}, u32[]{:S(2)}) collective-permute-start(f32[72,128]{1,0:T(8,128)S(1)} %add_add_fusion.3), channel_id=1, source_target_pairs={{0,20},{1,21},{2,22},{3,23},{4,16},{5,17},{6,18},{7,19},{8,28},{9,... | collective-permute-start | bytes 110600 | tf_op jit(solution)/shard_map/ppermute | solution.py:33
  19.4 4.9 %collective-permute-start.5 = (f32[72,128]{1,0:T(8,128)S(1)}, f32[72,128]{1,0:T(8,128)S(1)}, u32[]{:S(2)}, u32[]{:S(2)}) collective-permute-start(f32[72,128]{1,0:T(8,128)S(1)} %add_add_fusion.3), channel_id=1, source_target_pairs={{0,24},{1,25},{2,26},{3,27},{4,28},{5,29},{6,30},{7,31},{8,16},{9,... | collective-permute-start | bytes 110600 | tf_op jit(solution)/shard_map/ppermute | solution.py:33
  19.7 4.7 %collective-permute-start.4 = (f32[72,128]{1,0:T(8,128)S(1)}, f32[72,128]{1,0:T(8,128)S(1)}, u32[]{:S(2)}, u32[]{:S(2)}) collective-permute-start(f32[72,128]{1,0:T(8,128)S(1)} %add_add_fusion.3), channel_id=1, source_target_pairs={{0,8},{1,9},{2,10},{3,11},{4,12},{5,13},{6,14},{7,15},{8,0},{9,1},... | collective-permute-start | bytes 110600 | tf_op jit(solution)/shard_map/ppermute | solution.py:33
  24.4 4.4 %collective-permute-start.7 = (f32[72,128]{1,0:T(8,128)S(1)}, f32[72,128]{1,0:T(8,128)S(1)}, u32[]{:S(2)}, u32[]{:S(2)}) collective-permute-start(f32[72,128]{1,0:T(8,128)S(1)} %add_add_fusion.2.mine_ref), channel_id=1, source_target_pairs={{0,1},{1,0},{2,3},{3,2},{4,5},{5,4},{6,7},{7,6},{8,9},{9,8},{10,11... | collective-permute-start | bytes 110600 | tf_op jit(solution)/shard_map/ppermute | solution.py:33
  36.8 9.7 %collective-permute-start.8 = (f32[512,128]{1,0:T(8,128)S(1)}, f32[512,128]{1,0:T(8,128)S(1)}, u32[]{:S(2)}, u32[]{:S(2)}) collective-permute-start(f32[512,128]{1,0:T(8,128)S(1)} %get-tuple-element.10), channel_id=1, source_target_pairs={{224,0},{0,32},{32,64},{64,96},{96,128},{128,160},{160,192},{192,2... | collective-permute-start | bytes 786440 | tf_op jit(solution)/shard_map/ppermute | solution.py:233
  37.4 9.1 %collective-permute-start.9 = (f32[512,128]{1,0:T(8,128)S(1)}, f32[512,128]{1,0:T(8,128)S(1)}, u32[]{:S(2)}, u32[]{:S(2)}) collective-permute-start(f32[512,128]{1,0:T(8,128)S(1)} %get-tuple-element.11), channel_id=1, source_target_pairs={{32,0},{64,32},{96,64},{128,96},{160,128},{192,160},{224,192},{0,2... | collective-permute-start | bytes 786440 | tf_op jit(solution)/shard_map/ppermute | solution.py:233
  46.8 2.1 %collective-permute-start.10 = (f32[72,128]{1,0:T(8,128)S(1)}, f32[72,128]{1,0:T(8,128)S(1)}, u32[]{:S(2)}, u32[]{:S(2)}) collective-permute-start(f32[72,128]{1,0:T(8,128)S(1)} %get-tuple-element.13), channel_id=1, source_target_pairs={{0,1},{1,0},{2,3},{3,2},{4,5},{5,4},{6,7},{7,6},{8,9},{9,8},{10,11... | collective-permute-start | bytes 110600 | tf_op jit(solution)/shard_map/ppermute | solution.py:33
  49.0 5.2 %collective-permute-start.13 = (f32[72,128]{1,0:T(8,128)S(1)}, f32[72,128]{1,0:T(8,128)S(1)}, u32[]{:S(2)}, u32[]{:S(2)}) collective-permute-start(f32[72,128]{1,0:T(8,128)S(1)} %add.49), channel_id=1, source_target_pairs={{0,6},{1,7},{2,4},{3,5},{4,2},{5,3},{6,0},{7,1},{8,14},{9,15},{10,... | collective-permute-start | bytes 110600 | tf_op jit(solution)/shard_map/ppermute | solution.py:33
  49.6 4.5 %collective-permute-start.12 = (f32[72,128]{1,0:T(8,128)S(1)}, f32[72,128]{1,0:T(8,128)S(1)}, u32[]{:S(2)}, u32[]{:S(2)}) collective-permute-start(f32[72,128]{1,0:T(8,128)S(1)} %add.49), channel_id=1, source_target_pairs={{0,4},{1,5},{2,6},{3,7},{4,0},{5,1},{6,2},{7,3},{8,12},{9,13},{10,... | collective-permute-start | bytes 110600 | tf_op jit(solution)/shard_map/ppermute | solution.py:33
  50.4 4.7 %collective-permute-start.11 = (f32[72,128]{1,0:T(8,128)S(1)}, f32[72,128]{1,0:T(8,128)S(1)}, u32[]{:S(2)}, u32[]{:S(2)}) collective-permute-start(f32[72,128]{1,0:T(8,128)S(1)} %add.49), channel_id=1, source_target_pairs={{0,2},{1,3},{2,0},{3,1},{4,6},{5,7},{6,4},{7,5},{8,10},{9,11},{10,... | collective-permute-start | bytes 110600 | tf_op jit(solution)/shard_map/ppermute | solution.py:33
  55.1 5.9 %collective-permute-start.16 = (f32[72,128]{1,0:T(8,128)S(1)}, f32[72,128]{1,0:T(8,128)S(1)}, u32[]{:S(2)}, u32[]{:S(2)}) collective-permute-start(f32[72,128]{1,0:T(8,128)S(1)} %add_add_fusion.1), channel_id=1, source_target_pairs={{0,20},{1,21},{2,22},{3,23},{4,16},{5,17},{6,18},{7,19},{8,28},{9,... | collective-permute-start | bytes 110600 | tf_op jit(solution)/shard_map/ppermute | solution.py:33
  58.3 5.4 %collective-permute-start.15 = (f32[72,128]{1,0:T(8,128)S(1)}, f32[72,128]{1,0:T(8,128)S(1)}, u32[]{:S(2)}, u32[]{:S(2)}) collective-permute-start(f32[72,128]{1,0:T(8,128)S(1)} %add_add_fusion.1), channel_id=1, source_target_pairs={{0,24},{1,25},{2,26},{3,27},{4,28},{5,29},{6,30},{7,31},{8,16},{9,... | collective-permute-start | bytes 110600 | tf_op jit(solution)/shard_map/ppermute | solution.py:33
  59.2 4.8 %collective-permute-start.14 = (f32[72,128]{1,0:T(8,128)S(1)}, f32[72,128]{1,0:T(8,128)S(1)}, u32[]{:S(2)}, u32[]{:S(2)}) collective-permute-start(f32[72,128]{1,0:T(8,128)S(1)} %add_add_fusion.1), channel_id=1, source_target_pairs={{0,8},{1,9},{2,10},{3,11},{4,12},{5,13},{6,14},{7,15},{8,0},{9,1},... | collective-permute-start | bytes 110600 | tf_op jit(solution)/shard_map/ppermute | solution.py:33
  64.0 3.3 %collective-permute-start.17 = (f32[72,128]{1,0:T(8,128)S(1)}, f32[72,128]{1,0:T(8,128)S(1)}, u32[]{:S(2)}, u32[]{:S(2)}) collective-permute-start(f32[72,128]{1,0:T(8,128)S(1)} %add_add_fusion.mine_ref), channel_id=1, source_target_pairs={{0,1},{1,0},{2,3},{3,2},{4,5},{5,4},{6,7},{7,6},{8,9},{9,8},{10,11... | collective-permute-start | bytes 110600 | tf_op jit(solution)/shard_map/ppermute | solution.py:33

commit v3 on v2

v3 whole, which is shorter than its diff:
```python
import functools

import jax
import jax.numpy as jnp
from jax import lax
from jax.experimental import pallas as pl
from jax.experimental.pallas import tpu as pltpu
from jax.sharding import PartitionSpec as P

ROUNDS = 2
FIRST_LIMIT = 56_400_000
STAT_ROWS = 144
TOLERANCE = 1e-7

Z_PAIR = {0: 1, 2: 3, 4: 5, 6: 7}
Z_FAR = ({0: 5, 1: 4, 2: 7, 3: 6}, {0: 2, 1: 3, 4: 6, 5: 7}, {0: 6, 1: 7, 2: 4, 3: 5})


def both_ways(pairs):
    return {**pairs, **{b: a for a, b in pairs.items()}}


def row_route(z_map=None, flip_x=False, flip_core=False):
    route = []
    for i in range(32):
        z, x, core = i // 4, i // 2 % 2, i % 2
        z = both_ways(z_map)[z] if z_map else z
        route.append((i, z * 4 + (x ^ flip_x) * 2 + (core ^ flip_core)))
    return route


def across(value, **kinds):
    return lax.ppermute(value, "row", row_route(**kinds))


def on_core_0(value, otherwise):
    return jnp.where(lax.axis_index("row") % 2 == 0, value, otherwise)


def from_three(value, single, first, second):
    route = [r for r in row_route(**single) if r[0] % 2 == 0] + [r for r in row_route(**first) if r[0] % 2]
    added = lax.ppermute(value, "row", route)
    more = lax.ppermute(value, "row", [r for r in row_route(**second) if r[0] % 2])
    return on_core_0(value, more) + added


def with_other_core(value):
    return value + across(value, flip_core=True)


def summed_over_rows(value):
    value = with_other_core(value)
    value = from_three(value, dict(z_map=Z_PAIR, flip_x=True), dict(flip_x=True), dict(z_map=Z_PAIR))
    value = with_other_core(value)
    value = from_three(value, *(dict(z_map=pairs) for pairs in Z_FAR))
    return value, across(value, flip_core=True)


def split(value):
    high = value.astype(jnp.bfloat16)
    return high, (value - high.astype(jnp.float32)).astype(jnp.bfloat16)


def contract(a, b, dims):
    (ah, al), (bh, bl) = a, b
    dot = functools.partial(lax.dot_general, dimension_numbers=(dims, ((), ())), preferred_element_type=jnp.float32)
    return dot(ah, bh) + (dot(al, bh) + dot(ah, bl))


def exact_dot(a, b, dims=((1,), (0,))):
    return lax.dot_general(
        a, b, dimension_numbers=(dims, ((), ())), precision=lax.Precision.HIGHEST, preferred_element_type=jnp.float32
    )


def write_statistics(upper, lower, out_ref):
    width = upper.shape[1]
    out_ref[:width] = contract(split(upper), split(lower), ((0,), (0,)))
    for i, value in enumerate((upper, lower)):
        out_ref[pl.ds(width + 8 * i, 8)] = jnp.sum((value * value).reshape(-1, 8, width), axis=0)


VMEM = pl.BlockSpec(memory_space=pltpu.VMEM)
HBM = pl.BlockSpec(memory_space=pltpu.HBM)
PARAMS = pltpu.CompilerParams(vmem_limit_bytes=8 << 20)
PIECES = 4


def pieces_of(rows):
    return [pl.ds(i * (rows // PIECES), rows // PIECES) for i in range(PIECES)]


def stat_shape(width):
    return jax.ShapeDtypeStruct((STAT_ROWS, width), jnp.float32)


def first_kernel(upper_hbm, lower_hbm, sums_ref, upper_ref, lower_ref, sems):
    copies = [
        pltpu.make_async_copy(source.at[rows], target.at[rows], sems.at[i, j])
        for j, rows in enumerate(pieces_of(upper_hbm.shape[0]))
        for i, (source, target) in enumerate(((upper_hbm, upper_ref), (lower_hbm, lower_ref)))
    ]
    for copy in copies:
        copy.start()
    for copy in copies:
        copy.wait()
    write_statistics(upper_ref[...], lower_ref[...], sums_ref)


def first_statistics(upper, lower):
    return pl.pallas_call(
        first_kernel,
        out_shape=stat_shape(upper.shape[1]),
        in_specs=[HBM, HBM],
        out_specs=VMEM,
        scratch_shapes=[pltpu.VMEM(upper.shape, jnp.float32)] * 2 + [pltpu.SemaphoreType.DMA((2, PIECES))],
        compiler_params=pltpu.CompilerParams(vmem_limit_bytes=FIRST_LIMIT),
        name="first_statistics",
    )(upper, lower)


def statistics_kernel(upper_ref, lower_ref, sums_ref):
    write_statistics(upper_ref[...], lower_ref[...], sums_ref)


def statistics(upper, lower):
    return pl.pallas_call(
        statistics_kernel,
        out_shape=stat_shape(upper.shape[1]),
        in_specs=[VMEM, VMEM],
        out_specs=VMEM,
        compiler_params=PARAMS,
        name="statistics",
    )(upper, lower)


def coupling_of(sums, row_total):
    width = sums.shape[1]
    sums = sums * (1.0 / row_total)
    cross_gram = sums[:width]
    upper_norms = jnp.sum(sums[width : width + 8], axis=0, keepdims=True)
    lower_norms = jnp.sum(sums[width + 8 :], axis=0, keepdims=True)
    upper_norms = jnp.broadcast_to(upper_norms, (width, width)).T
    gap = upper_norms - lower_norms
    both = upper_norms + lower_norms
    return -cross_gram * gap / (2.0 * gap * gap + 0.5 * both * both + 1e-05)


def solved(coupling, residual_ref, result_ref):
    width = coupling.shape[0]
    identity = (
        lax.broadcasted_iota(jnp.int32, (width, width), 0) == lax.broadcasted_iota(jnp.int32, (width, width), 1)
    ).astype(jnp.float32)
    parts = split(coupling)
    outer = contract(parts, parts, ((1,), (1,)))
    size = jnp.sqrt(jnp.sum(jnp.sum(outer * outer, axis=0, keepdims=True), axis=1, keepdims=True))
    alpha = 2.0 / (2.0 + size)
    bound = jnp.sum(size / (2.0 + size))
    residual = (1.0 - alpha) * identity - alpha * outer

    def series(right):
        parts = split(residual)
        right = right + contract(parts, split(right), ((1,), (0,)))
        square = contract(parts, parts, ((1,), (0,)))
        residual_ref[...] = square
        result_ref[...] = right + contract(split(square), split(right), ((1,), (0,)))

        def factor(bound):
            square = exact_dot(residual_ref[...], residual_ref[...])
            residual_ref[...] = square
            result_ref[...] += exact_dot(square, result_ref[...])
            return bound * bound

        lax.while_loop(lambda bound: bound > TOLERANCE, factor, (bound * bound) * (bound * bound))

    series((2.0 * alpha) * coupling)

    @pl.when(bound > 0.5)
    def _():
        exact_outer = exact_dot(coupling, coupling, ((1,), (1,)))
        for _ in range(2):
            value = result_ref[...]
            series(alpha * ((2.0 * coupling - value) - exact_dot(exact_outer, value)))
            result_ref[...] += value

    return result_ref[...]


def apply(upper, lower, change):
    return contract(split(jnp.concatenate([upper, lower], axis=1)), change, ((1,), (0,)))


def full_change(coupling, to_lower):
    both = (split(coupling), split(to_lower))
    upper_loss = contract(*both, ((1,), (1,)))
    lower_loss = contract(*both, ((0,), (0,)))
    return split(
        jnp.concatenate(
            [
                jnp.concatenate([-upper_loss, to_lower], axis=1),
                jnp.concatenate([-to_lower.T, -lower_loss], axis=1),
            ],
            axis=0,
        )
    )


def last_kernel(row_total, mine_ref, other_ref, upper_ref, lower_ref, upper_hbm, lower_hbm, residual_ref, result_ref,
                new_upper_ref, new_lower_ref, sems):
    coupling = coupling_of(mine_ref[...] + other_ref[...], row_total)
    to_lower = solved(coupling, residual_ref, result_ref)
    change = full_change(coupling, to_lower)
    width = upper_ref.shape[1]
    copies = []
    for j, rows in enumerate(pieces_of(upper_ref.shape[0])):
        moved = apply(upper_ref[rows], lower_ref[rows], change)
        new_upper_ref[rows] = upper_ref[rows] + moved[:, :width]
        new_lower_ref[rows] = lower_ref[rows] + moved[:, width:]
        for i, (source, target) in enumerate(((new_upper_ref, upper_hbm), (new_lower_ref, lower_hbm))):
            copies.append(pltpu.make_async_copy(source.at[rows], target.at[rows], sems.at[i, j]))
            copies[-1].start()
    for copy in copies:
        copy.wait()


def rotated_last(mine, other, upper, lower, row_total):
    width = upper.shape[1]
    square = pltpu.VMEM((width, width), jnp.float32)
    return pl.pallas_call(
        functools.partial(last_kernel, row_total),
        out_shape=(jax.ShapeDtypeStruct(upper.shape, jnp.float32),) * 2,
        in_specs=[VMEM] * 4,
        out_specs=(HBM, HBM),
        scratch_shapes=[square, square]
        + [pltpu.VMEM(upper.shape, jnp.float32)] * 2
        + [pltpu.SemaphoreType.DMA((2, PIECES))],
        compiler_params=PARAMS,
        name="rotate_last",
    )(mine, other, upper, lower)


def rotate_kernel(row_total, mine_ref, other_ref, upper_ref, lower_ref, new_upper_ref, new_lower_ref, residual_ref, result_ref):
    coupling = coupling_of(mine_ref[...] + other_ref[...], row_total)
    to_lower = solved(coupling, residual_ref, result_ref)
    width = upper_ref.shape[1]
    moved = apply(upper_ref[...], lower_ref[...], full_change(coupling, to_lower))
    new_upper_ref[...] = upper_ref[...] + moved[:, :width]
    new_lower_ref[...] = lower_ref[...] + moved[:, width:]


def rotated(mine, other, upper, lower, row_total):
    width = upper.shape[1]
    return pl.pallas_call(
        functools.partial(rotate_kernel, row_total),
        out_shape=(jax.ShapeDtypeStruct(upper.shape, jnp.float32),) * 2,
        in_specs=[VMEM] * 4,
        out_specs=(VMEM, VMEM),
        scratch_shapes=[pltpu.VMEM((width, width), jnp.float32)] * 2,
        compiler_params=PARAMS,
        name="rotate",
    )(mine, other, upper, lower)


def from_behind(block, distance):
    devices = lax.axis_size("col")
    return lax.ppermute(block, "col", [((i - distance) % devices, i) for i in range(devices)])


def shards(upper, lower):
    row_total = float(upper.shape[0] * lax.axis_size("row"))
    mine, other = summed_over_rows(first_statistics(upper, lower))
    upper, lower = rotated(mine, other, upper, lower, row_total)
    upper, lower = from_behind(upper, 1), from_behind(lower, -1)
    mine, other = summed_over_rows(statistics(upper, lower))
    return rotated_last(mine, other, upper, lower, row_total)


def solution(mesh):
    placed = (P("row", "col"), P("row", "col"))
    return jax.shard_map(shards, mesh=mesh, in_specs=placed, out_specs=placed, check_vma=False)
```

time: 76.4 us -> 79.1 us (1.035)
  Pallas kernels: 18.4 us -> 22.8 us
  starting transfers between devices: 35.3 us -> 33.9 us
    ppermute x16 -> x6, starting transfers between devices: 31.7 us -> 5.58 us  [across(): return lax.ppermute(value, 'row', row_route(**kinds))]
    ppermute x0 -> x8, starting transfers between devices: none -> 24.7 us  [the longest x4 16.9 us: from_three(): lax.ppermute(value, 'row', [r for r in row_route(**second) if r[0] % 2])]
    ppermute x16 -> x6, waiting for transfers between devices: 15.3 us -> 6.21 us  [across(): return lax.ppermute(value, 'row', row_route(**kinds))]
    ppermute x0 -> x8, waiting for transfers between devices: none -> 8.9 us  [the longest x4 8.74 us: from_three(): lax.ppermute(value, 'row', [r for r in row_route(**second) if r[0] % 2])]
    pallas_call x4, Pallas kernels: 18.4 us -> 22.8 us  [the longest x1 11.6 us: rotated_last(): pl.pallas_call(functools.partial(last_kernel, row_total), out_shape=(jax....]
  transfers between devices with their start and end apart: 18 -> 16, of which waited for: 15 -> 12; matrix products, arithmetic and copies ran while one was open for 0% -> 0% of each run, Pallas kernels for 0% -> 0%
where the time goes in v3:
time: 79.1 us; the launch traced here: 79 us
  starting transfers between devices  33.9 us (43%)
  Pallas kernels  22.8 us (29%)
  waiting for transfers between devices  21.4 us (27%)
    ppermute x4, starting transfers between devices, from_three(): lax.ppermute(value, 'row', [r for r in row_route(**second) if r[0] % 2])  16.9 us
    pallas_call x1, Pallas kernels, rotated_last(): pl.pallas_call(functools.partial(last_kernel, row_total), out_shape=(jax....  11.6 us
    pallas_call x1, Pallas kernels, rotated(): pl.pallas_call(functools.partial(rotate_kernel, row_total), out_shape=(ja...  9.5 us
    ppermute x4, waiting for transfers between devices, from_three(): lax.ppermute(value, 'row', [r for r in row_route(**second) if r[0] % 2])  8.74 us
    ppermute x4, starting transfers between devices, from_three(): added = lax.ppermute(value, 'row', route)  7.82 us
    ppermute x2, waiting for transfers between devices, from_behind(): lax.ppermute(block, 'col', [((i - distance) % devices, i) for i in range(...  6.29 us
    ppermute x6, waiting for transfers between devices, across(): return lax.ppermute(value, 'row', row_route(**kinds))  6.21 us
    ppermute x6, starting transfers between devices, across(): return lax.ppermute(value, 'row', row_route(**kinds))  5.58 us
  transfers between devices with their start and end apart: 16, of which 12 were waited for; matrix products, arithmetic and copies ran while one was open for 0% of the time, Pallas kernels for 0%

profile of v3, /device:TPU:1, one launch (start us, length us, event | category | flops | bytes accessed | tf_op | source)
XLA Modules:
  0.0 79.0 jit_solution(6833766710992719191)
XLA Ops:
  0.6 1.4 %first_statistics.1 = f32[144,128]{1,0:T(8,128)S(1)} custom-call(f32[512,128]{1,0:T(8,128)} %upper_ref.1, f32[512,128]{1,0:T(8,128)} %lower_ref.1), custom_call_target="tpu_custom_call" | custom-call | tf_op jit(solution)/shard_map/first_statistics/pallas_call | solution.py:111
  2.1 3.3 %collective-permute-start = (f32[144,128]{1,0:T(8,128)S(1)}, f32[144,128]{1,0:T(8,128)S(1)}, u32[]{:S(2)}, u32[]{:S(2)}) collective-permute-start(f32[144,128]{1,0:T(8,128)S(1)} %first_statistics.1), channel_id=1, source_target_pairs={{0,1},{1,0},{2,3},{3,2},{4,5},{5,4},{6,7},{7,6},{8,9},{9,8},{10,11... | collective-permute-start | bytes 221192 | tf_op jit(solution)/shard_map/ppermute | solution.py:33
  5.4 0.9 %collective-permute-done = f32[144,128]{1,0:T(8,128)S(1)} collective-permute-done((f32[144,128]{1,0:T(8,128)S(1)}, f32[144,128]{1,0:T(8,128)S(1)}, u32[]{:S(2)}, u32[]{:S(2)}) %collective-permute-start) | collective-permute-done | bytes 73760 | tf_op jit(solution)/shard_map/ppermute | solution.py:33
  6.3 1.1 %collective-permute-start.2 = (f32[144,128]{1,0:T(8,128)S(1)}, f32[144,128]{1,0:T(8,128)S(1)}, u32[]{:S(2)}, u32[]{:S(2)}) collective-permute-start(f32[144,128]{1,0:T(8,128)S(1)} %add.32), channel_id=1, source_target_pairs={{0,6},{2,4},{4,2},{6,0},{8,14},{10,12},{12,10},{14,8},{16,22},{18,... | collective-permute-start | bytes 221192 | tf_op jit(solution)/shard_map/ppermute | solution.py:42
  7.4 3.5 %collective-permute-start.1 = (f32[144,128]{1,0:T(8,128)S(1)}, f32[144,128]{1,0:T(8,128)S(1)}, u32[]{:S(2)}, u32[]{:S(2)}) collective-permute-start(f32[144,128]{1,0:T(8,128)S(1)} %add.32), channel_id=1, source_target_pairs={{1,5},{3,7},{5,1},{7,3},{9,13},{11,15},{13,9},{15,11},{17,21},{19,... | collective-permute-start | bytes 221192 | tf_op jit(solution)/shard_map/ppermute | solution.py:43
  11.0 0.1 collective-permute-done.2
  11.1 1.9 %collective-permute-done.1 = f32[144,128]{1,0:T(8,128)S(1)} collective-permute-done((f32[144,128]{1,0:T(8,128)S(1)}, f32[144,128]{1,0:T(8,128)S(1)}, u32[]{:S(2)}, u32[]{:S(2)}) %collective-permute-start.1) | collective-permute-done | bytes 73760 | tf_op jit(solution)/shard_map/ppermute | solution.py:43
  13.0 0.0 copy-start.1
  13.0 0.0 copy-start
  13.0 0.6 collective-permute-start.3
  13.7 0.9 %collective-permute-done.3 = f32[144,128]{1,0:T(8,128)S(1)} collective-permute-done((f32[144,128]{1,0:T(8,128)S(1)}, f32[144,128]{1,0:T(8,128)S(1)}, u32[]{:S(2)}, u32[]{:S(2)}) %collective-permute-start.3) | collective-permute-done | bytes 73760 | tf_op jit(solution)/shard_map/ppermute | solution.py:33
  14.6 2.6 %collective-permute-start.5 = (f32[144,128]{1,0:T(8,128)S(1)}, f32[144,128]{1,0:T(8,128)S(1)}, u32[]{:S(2)}, u32[]{:S(2)}) collective-permute-start(f32[144,128]{1,0:T(8,128)S(1)} %add.34), channel_id=1, source_target_pairs={{0,20},{2,22},{4,16},{6,18},{8,28},{10,30},{12,24},{14,26},{16,4},... | collective-permute-start | bytes 221192 | tf_op jit(solution)/shard_map/ppermute | solution.py:42
  17.2 5.9 %collective-permute-start.4 = (f32[144,128]{1,0:T(8,128)S(1)}, f32[144,128]{1,0:T(8,128)S(1)}, u32[]{:S(2)}, u32[]{:S(2)}) collective-permute-start(f32[144,128]{1,0:T(8,128)S(1)} %add.34), channel_id=1, source_target_pairs={{1,25},{3,27},{5,29},{7,31},{9,17},{11,19},{13,21},{15,23},{17,9},... | collective-permute-start | bytes 221192 | tf_op jit(solution)/shard_map/ppermute | solution.py:43
  23.1 0.0 collective-permute-done.5
  23.1 2.1 %collective-permute-done.4 = f32[144,128]{1,0:T(8,128)S(1)} collective-permute-done((f32[144,128]{1,0:T(8,128)S(1)}, f32[144,128]{1,0:T(8,128)S(1)}, u32[]{:S(2)}, u32[]{:S(2)}) %collective-permute-start.4) | collective-permute-done | bytes 73760 | tf_op jit(solution)/shard_map/ppermute | solution.py:43
  25.2 0.1 collective-permute-start.6
  25.3 1.3 %collective-permute-done.6.other_ref = f32[144,128]{1,0:T(8,128)S(1)} collective-permute-done((f32[144,128]{1,0:T(8,128)S(1)}, f32[144,128]{1,0:T(8,128)S(1)}, u32[]{:S(2)}, u32[]{:S(2)}) %collective-permute-start.6) | collective-permute-done | bytes 73760 | tf_op jit(solution)/shard_map/ppermute | solution.py:33
  26.5 0.0 copy-done.1
  26.5 0.0 copy-done
  26.5 9.5 %rotate.1 = (f32[512,128]{1,0:T(8,128)S(1)}, f32[512,128]{1,0:T(8,128)S(1)}) custom-call(f32[144,128]{1,0:T(8,128)S(1)} %select_add_fusion.2.mine_ref, f32[144,128]{1,0:T(8,128)S(1)} %collective-permute-done.6.other_ref, f32[512,128]{1,0:T(8,128)S(1)} %copy-done, f32[512,128]{1,0:T(8,128)S(1)} %copy-done.1), custom_call_target="tpu_custom_call" | custom-call | tf_op jit(solution)/shard_map/rotate/pallas_call | solution.py:253
  36.0 1.4 %collective-permute-start.7 = (f32[512,128]{1,0:T(8,128)S(1)}, f32[512,128]{1,0:T(8,128)S(1)}, u32[]{:S(2)}, u32[]{:S(2)}) collective-permute-start(f32[512,128]{1,0:T(8,128)S(1)} %get-tuple-element.4), channel_id=1, source_target_pairs={{224,0},{0,32},{32,64},{64,96},{96,128},{128,160},{160,192},{192,2... | collective-permute-start | bytes 786440 | tf_op jit(solution)/shard_map/ppermute | solution.py:266
  37.4 2.3 %collective-permute-start.8 = (f32[512,128]{1,0:T(8,128)S(1)}, f32[512,128]{1,0:T(8,128)S(1)}, u32[]{:S(2)}, u32[]{:S(2)}) collective-permute-start(f32[512,128]{1,0:T(8,128)S(1)} %get-tuple-element.5), channel_id=1, source_target_pairs={{32,0},{64,32},{96,64},{128,96},{160,128},{192,160},{224,192},{0,2... | collective-permute-start | bytes 786440 | tf_op jit(solution)/shard_map/ppermute | solution.py:266
  39.7 6.3 %collective-permute-done.7.upper_ref = f32[512,128]{1,0:T(8,128)S(1)} collective-permute-done((f32[512,128]{1,0:T(8,128)S(1)}, f32[512,128]{1,0:T(8,128)S(1)}, u32[]{:S(2)}, u32[]{:S(2)}) %collective-permute-start.7) | collective-permute-done | bytes 262176 | tf_op jit(solution)/shard_map/ppermute | solution.py:266
  46.0 0.0 collective-permute-done.8.lower_ref
  46.0 0.3 statistics.1
  46.3 1.1 %collective-permute-start.9 = (f32[144,128]{1,0:T(8,128)S(1)}, f32[144,128]{1,0:T(8,128)S(1)}, u32[]{:S(2)}, u32[]{:S(2)}) collective-permute-start(f32[144,128]{1,0:T(8,128)S(1)} %statistics.1), channel_id=1, source_target_pairs={{0,1},{1,0},{2,3},{3,2},{4,5},{5,4},{6,7},{7,6},{8,9},{9,8},{10,11... | collective-permute-start | bytes 221192 | tf_op jit(solution)/shard_map/ppermute | solution.py:33
  47.4 0.9 %collective-permute-done.9 = f32[144,128]{1,0:T(8,128)S(1)} collective-permute-done((f32[144,128]{1,0:T(8,128)S(1)}, f32[144,128]{1,0:T(8,128)S(1)}, u32[]{:S(2)}, u32[]{:S(2)}) %collective-permute-start.9) | collective-permute-done | bytes 73760 | tf_op jit(solution)/shard_map/ppermute | solution.py:33
  48.3 1.8 %collective-permute-start.11 = (f32[144,128]{1,0:T(8,128)S(1)}, f32[144,128]{1,0:T(8,128)S(1)}, u32[]{:S(2)}, u32[]{:S(2)}) collective-permute-start(f32[144,128]{1,0:T(8,128)S(1)} %add.36), channel_id=1, source_target_pairs={{0,6},{2,4},{4,2},{6,0},{8,14},{10,12},{12,10},{14,8},{16,22},{18,... | collective-permute-start | bytes 221192 | tf_op jit(solution)/shard_map/ppermute | solution.py:42
  50.1 3.3 %collective-permute-start.10 = (f32[144,128]{1,0:T(8,128)S(1)}, f32[144,128]{1,0:T(8,128)S(1)}, u32[]{:S(2)}, u32[]{:S(2)}) collective-permute-start(f32[144,128]{1,0:T(8,128)S(1)} %add.36), channel_id=1, source_target_pairs={{1,5},{3,7},{5,1},{7,3},{9,13},{11,15},{13,9},{15,11},{17,21},{19,... | collective-permute-start | bytes 221192 | tf_op jit(solution)/shard_map/ppermute | solution.py:43
  53.4 0.0 collective-permute-done.11
  53.4 1.8 %collective-permute-done.10 = f32[144,128]{1,0:T(8,128)S(1)} collective-permute-done((f32[144,128]{1,0:T(8,128)S(1)}, f32[144,128]{1,0:T(8,128)S(1)}, u32[]{:S(2)}, u32[]{:S(2)}) %collective-permute-start.10) | collective-permute-done | bytes 73760 | tf_op jit(solution)/shard_map/ppermute | solution.py:43
  55.2 0.4 collective-permute-start.12
  55.6 1.0 %collective-permute-done.12 = f32[144,128]{1,0:T(8,128)S(1)} collective-permute-done((f32[144,128]{1,0:T(8,128)S(1)}, f32[144,128]{1,0:T(8,128)S(1)}, u32[]{:S(2)}, u32[]{:S(2)}) %collective-permute-start.12) | collective-permute-done | bytes 73760 | tf_op jit(solution)/shard_map/ppermute | solution.py:33
  56.6 2.3 %collective-permute-start.14 = (f32[144,128]{1,0:T(8,128)S(1)}, f32[144,128]{1,0:T(8,128)S(1)}, u32[]{:S(2)}, u32[]{:S(2)}) collective-permute-start(f32[144,128]{1,0:T(8,128)S(1)} %add.38), channel_id=1, source_target_pairs={{0,20},{2,22},{4,16},{6,18},{8,28},{10,30},{12,24},{14,26},{16,4},... | collective-permute-start | bytes 221192 | tf_op jit(solution)/shard_map/ppermute | solution.py:42
  58.9 4.1 %collective-permute-start.13 = (f32[144,128]{1,0:T(8,128)S(1)}, f32[144,128]{1,0:T(8,128)S(1)}, u32[]{:S(2)}, u32[]{:S(2)}) collective-permute-start(f32[144,128]{1,0:T(8,128)S(1)} %add.38), channel_id=1, source_target_pairs={{1,25},{3,27},{5,29},{7,31},{9,17},{11,19},{13,21},{15,23},{17,9},... | collective-permute-start | bytes 221192 | tf_op jit(solution)/shard_map/ppermute | solution.py:43
  63.0 0.0 collective-permute-done.14
  63.1 3.0 %collective-permute-done.13 = f32[144,128]{1,0:T(8,128)S(1)} collective-permute-done((f32[144,128]{1,0:T(8,128)S(1)}, f32[144,128]{1,0:T(8,128)S(1)}, u32[]{:S(2)}, u32[]{:S(2)}) %collective-permute-start.13) | collective-permute-done | bytes 73760 | tf_op jit(solution)/shard_map/ppermute | solution.py:43
  66.1 0.1 collective-permute-start.15
  66.2 1.3 %collective-permute-done.15.other_ref = f32[144,128]{1,0:T(8,128)S(1)} collective-permute-done((f32[144,128]{1,0:T(8,128)S(1)}, f32[144,128]{1,0:T(8,128)S(1)}, u32[]{:S(2)}, u32[]{:S(2)}) %collective-permute-start.15) | collective-permute-done | bytes 73760 | tf_op jit(solution)/shard_map/ppermute | solution.py:33
  67.5 11.6 %rotate_last.1 = (f32[512,128]{1,0:T(8,128)}, f32[512,128]{1,0:T(8,128)}) custom-call(f32[144,128]{1,0:T(8,128)S(1)} %select_add_fusion.mine_ref, f32[144,128]{1,0:T(8,128)S(1)} %collective-permute-done.15.other_ref, f32[512,128]{1,0:T(8,128)S(1)} %collective-permute-done.7.upper_ref, f32[512,128]{1,0:T(8,128)S(1)} %collective-permute-done.8.lower_ref), custom_call_target="tpu_custom_call" | custom-call | tf_op jit(solution)/shard_map/rotate_last/pallas_call | solution.py:229
  (8 shorter events, 0.1 us)
Async XLA Ops:
  2.1 4.2 %collective-permute-start = (f32[144,128]{1,0:T(8,128)S(1)}, f32[144,128]{1,0:T(8,128)S(1)}, u32[]{:S(2)}, u32[]{:S(2)}) collective-permute-start(f32[144,128]{1,0:T(8,128)S(1)} %first_statistics.1), channel_id=1, source_target_pairs={{0,1},{1,0},{2,3},{3,2},{4,5},{5,4},{6,7},{7,6},{8,9},{9,8},{10,11... | collective-permute-start | bytes 221192 | tf_op jit(solution)/shard_map/ppermute | solution.py:33
  6.3 4.8 %collective-permute-start.2 = (f32[144,128]{1,0:T(8,128)S(1)}, f32[144,128]{1,0:T(8,128)S(1)}, u32[]{:S(2)}, u32[]{:S(2)}) collective-permute-start(f32[144,128]{1,0:T(8,128)S(1)} %add.32), channel_id=1, source_target_pairs={{0,6},{2,4},{4,2},{6,0},{8,14},{10,12},{12,10},{14,8},{16,22},{18,... | collective-permute-start | bytes 221192 | tf_op jit(solution)/shard_map/ppermute | solution.py:42
  7.4 5.6 %collective-permute-start.1 = (f32[144,128]{1,0:T(8,128)S(1)}, f32[144,128]{1,0:T(8,128)S(1)}, u32[]{:S(2)}, u32[]{:S(2)}) collective-permute-start(f32[144,128]{1,0:T(8,128)S(1)} %add.32), channel_id=1, source_target_pairs={{1,5},{3,7},{5,1},{7,3},{9,13},{11,15},{13,9},{15,11},{17,21},{19,... | collective-permute-start | bytes 221192 | tf_op jit(solution)/shard_map/ppermute | solution.py:43
  13.0 13.5 %copy-start.1 = (f32[512,128]{1,0:T(8,128)S(1)}, f32[512,128]{1,0:T(8,128)}, u32[]{:S(2)}) copy-start(f32[512,128]{1,0:T(8,128)} %lower_ref.1) | copy-start | bytes 786436
  13.0 13.5 %copy-start = (f32[512,128]{1,0:T(8,128)S(1)}, f32[512,128]{1,0:T(8,128)}, u32[]{:S(2)}) copy-start(f32[512,128]{1,0:T(8,128)} %upper_ref.1) | copy-start | bytes 786436
  13.0 1.5 %collective-permute-start.3 = (f32[144,128]{1,0:T(8,128)S(1)}, f32[144,128]{1,0:T(8,128)S(1)}, u32[]{:S(2)}, u32[]{:S(2)}) collective-permute-start(f32[144,128]{1,0:T(8,128)S(1)} %select_add_fusion.3), channel_id=1, source_target_pairs={{0,1},{1,0},{2,3},{3,2},{4,5},{5,4},{6,7},{7,6},{8,9},{9,8},{10,11... | collective-permute-start | bytes 221192 | tf_op jit(solution)/shard_map/ppermute | solution.py:33
  14.6 8.5 %collective-permute-start.5 = (f32[144,128]{1,0:T(8,128)S(1)}, f32[144,128]{1,0:T(8,128)S(1)}, u32[]{:S(2)}, u32[]{:S(2)}) collective-permute-start(f32[144,128]{1,0:T(8,128)S(1)} %add.34), channel_id=1, source_target_pairs={{0,20},{2,22},{4,16},{6,18},{8,28},{10,30},{12,24},{14,26},{16,4},... | collective-permute-start | bytes 221192 | tf_op jit(solution)/shard_map/ppermute | solution.py:42
  17.2 8.0 %collective-permute-start.4 = (f32[144,128]{1,0:T(8,128)S(1)}, f32[144,128]{1,0:T(8,128)S(1)}, u32[]{:S(2)}, u32[]{:S(2)}) collective-permute-start(f32[144,128]{1,0:T(8,128)S(1)} %add.34), channel_id=1, source_target_pairs={{1,25},{3,27},{5,29},{7,31},{9,17},{11,19},{13,21},{15,23},{17,9},... | collective-permute-start | bytes 221192 | tf_op jit(solution)/shard_map/ppermute | solution.py:43
  25.2 1.4 %collective-permute-start.6 = (f32[144,128]{1,0:T(8,128)S(1)}, f32[144,128]{1,0:T(8,128)S(1)}, u32[]{:S(2)}, u32[]{:S(2)}) collective-permute-start(f32[144,128]{1,0:T(8,128)S(1)} %select_add_fusion.2.mine_ref), channel_id=1, source_target_pairs={{0,1},{1,0},{2,3},{3,2},{4,5},{5,4},{6,7},{7,6},{8,9},{9,8},{10,11... | collective-permute-start | bytes 221192 | tf_op jit(solution)/shard_map/ppermute | solution.py:33
  36.0 9.9 %collective-permute-start.7 = (f32[512,128]{1,0:T(8,128)S(1)}, f32[512,128]{1,0:T(8,128)S(1)}, u32[]{:S(2)}, u32[]{:S(2)}) collective-permute-start(f32[512,128]{1,0:T(8,128)S(1)} %get-tuple-element.4), channel_id=1, source_target_pairs={{224,0},{0,32},{32,64},{64,96},{96,128},{128,160},{160,192},{192,2... | collective-permute-start | bytes 786440 | tf_op jit(solution)/shard_map/ppermute | solution.py:266
  37.4 8.6 %collective-permute-start.8 = (f32[512,128]{1,0:T(8,128)S(1)}, f32[512,128]{1,0:T(8,128)S(1)}, u32[]{:S(2)}, u32[]{:S(2)}) collective-permute-start(f32[512,128]{1,0:T(8,128)S(1)} %get-tuple-element.5), channel_id=1, source_target_pairs={{32,0},{64,32},{96,64},{128,96},{160,128},{192,160},{224,192},{0,2... | collective-permute-start | bytes 786440 | tf_op jit(solution)/shard_map/ppermute | solution.py:266
  46.3 2.0 %collective-permute-start.9 = (f32[144,128]{1,0:T(8,128)S(1)}, f32[144,128]{1,0:T(8,128)S(1)}, u32[]{:S(2)}, u32[]{:S(2)}) collective-permute-start(f32[144,128]{1,0:T(8,128)S(1)} %statistics.1), channel_id=1, source_target_pairs={{0,1},{1,0},{2,3},{3,2},{4,5},{5,4},{6,7},{7,6},{8,9},{9,8},{10,11... | collective-permute-start | bytes 221192 | tf_op jit(solution)/shard_map/ppermute | solution.py:33
  48.3 5.1 %collective-permute-start.11 = (f32[144,128]{1,0:T(8,128)S(1)}, f32[144,128]{1,0:T(8,128)S(1)}, u32[]{:S(2)}, u32[]{:S(2)}) collective-permute-start(f32[144,128]{1,0:T(8,128)S(1)} %add.36), channel_id=1, source_target_pairs={{0,6},{2,4},{4,2},{6,0},{8,14},{10,12},{12,10},{14,8},{16,22},{18,... | collective-permute-start | bytes 221192 | tf_op jit(solution)/shard_map/ppermute | solution.py:42
  50.1 5.1 %collective-permute-start.10 = (f32[144,128]{1,0:T(8,128)S(1)}, f32[144,128]{1,0:T(8,128)S(1)}, u32[]{:S(2)}, u32[]{:S(2)}) collective-permute-start(f32[144,128]{1,0:T(8,128)S(1)} %add.36), channel_id=1, source_target_pairs={{1,5},{3,7},{5,1},{7,3},{9,13},{11,15},{13,9},{15,11},{17,21},{19,... | collective-permute-start | bytes 221192 | tf_op jit(solution)/shard_map/ppermute | solution.py:43
  55.2 1.4 %collective-permute-start.12 = (f32[144,128]{1,0:T(8,128)S(1)}, f32[144,128]{1,0:T(8,128)S(1)}, u32[]{:S(2)}, u32[]{:S(2)}) collective-permute-start(f32[144,128]{1,0:T(8,128)S(1)} %select_add_fusion.1), channel_id=1, source_target_pairs={{0,1},{1,0},{2,3},{3,2},{4,5},{5,4},{6,7},{7,6},{8,9},{9,8},{10,11... | collective-permute-start | bytes 221192 | tf_op jit(solution)/shard_map/ppermute | solution.py:33
  56.6 6.5 %collective-permute-start.14 = (f32[144,128]{1,0:T(8,128)S(1)}, f32[144,128]{1,0:T(8,128)S(1)}, u32[]{:S(2)}, u32[]{:S(2)}) collective-permute-start(f32[144,128]{1,0:T(8,128)S(1)} %add.38), channel_id=1, source_target_pairs={{0,20},{2,22},{4,16},{6,18},{8,28},{10,30},{12,24},{14,26},{16,4},... | collective-permute-start | bytes 221192 | tf_op jit(solution)/shard_map/ppermute | solution.py:42
  58.9 7.2 %collective-permute-start.13 = (f32[144,128]{1,0:T(8,128)S(1)}, f32[144,128]{1,0:T(8,128)S(1)}, u32[]{:S(2)}, u32[]{:S(2)}) collective-permute-start(f32[144,128]{1,0:T(8,128)S(1)} %add.38), channel_id=1, source_target_pairs={{1,25},{3,27},{5,29},{7,31},{9,17},{11,19},{13,21},{15,23},{17,9},... | collective-permute-start | bytes 221192 | tf_op jit(solution)/shard_map/ppermute | solution.py:43
  66.1 1.4 %collective-permute-start.15 = (f32[144,128]{1,0:T(8,128)S(1)}, f32[144,128]{1,0:T(8,128)S(1)}, u32[]{:S(2)}, u32[]{:S(2)}) collective-permute-start(f32[144,128]{1,0:T(8,128)S(1)} %select_add_fusion.mine_ref), channel_id=1, source_target_pairs={{0,1},{1,0},{2,3},{3,2},{4,5},{5,4},{6,7},{7,6},{8,9},{9,8},{10,11... | collective-permute-start | bytes 221192 | tf_op jit(solution)/shard_map/ppermute | solution.py:33

commit v4 on v3

--- a/solution.py
+++ b/solution.py
@@ -9,7 +9,7 @@
 
 ROUNDS = 2
 FIRST_LIMIT = 56_400_000
-STAT_ROWS = 144
+STAT_ROWS = 136
 TOLERANCE = 1e-7
 
 Z_PAIR = {0: 1, 2: 3, 4: 5, 6: 7}
@@ -50,9 +50,9 @@
 
 def summed_over_rows(value):
     value = with_other_core(value)
+    value = from_three(value, *(dict(z_map=pairs) for pairs in Z_FAR))
+    value = with_other_core(value)
     value = from_three(value, dict(z_map=Z_PAIR, flip_x=True), dict(flip_x=True), dict(z_map=Z_PAIR))
-    value = with_other_core(value)
-    value = from_three(value, *(dict(z_map=pairs) for pairs in Z_FAR))
     return value, across(value, flip_core=True)
 
 
@@ -73,11 +73,18 @@
     )
 
 
-def write_statistics(upper, lower, out_ref):
-    width = upper.shape[1]
-    out_ref[:width] = contract(split(upper), split(lower), ((0,), (0,)))
-    for i, value in enumerate((upper, lower)):
-        out_ref[pl.ds(width + 8 * i, 8)] = jnp.sum((value * value).reshape(-1, 8, width), axis=0)
+def partial_statistics(upper, lower):
+    squares = [jnp.sum((v * v).reshape(-1, 8, v.shape[1]), axis=0) for v in (upper, lower)]
+    return [contract(split(upper), split(lower), ((0,), (0,))), *squares]
+
+
+def write_statistics(parts, out_ref):
+    gram, *squares = parts
+    width = gram.shape[0]
+    out_ref[:width] = gram
+    sums = [jnp.broadcast_to(jnp.sum(s, axis=0, keepdims=True), s.shape) for s in squares]
+    is_upper = lax.broadcasted_iota(jnp.int32, sums[0].shape, 0) < 4
+    out_ref[width:] = jnp.where(is_upper, *sums)
 
 
 VMEM = pl.BlockSpec(memory_space=pltpu.VMEM)
@@ -104,7 +111,7 @@
         copy.start()
     for copy in copies:
         copy.wait()
-    write_statistics(upper_ref[...], lower_ref[...], sums_ref)
+    write_statistics(partial_statistics(upper_ref[...], lower_ref[...]), sums_ref)
 
 
 def first_statistics(upper, lower):
@@ -120,7 +127,7 @@
 
 
 def statistics_kernel(upper_ref, lower_ref, sums_ref):
-    write_statistics(upper_ref[...], lower_ref[...], sums_ref)
+    write_statistics(partial_statistics(upper_ref[...], lower_ref[...]), sums_ref)
 
 
 def statistics(upper, lower):
@@ -138,8 +145,7 @@
     width = sums.shape[1]
     sums = sums * (1.0 / row_total)
     cross_gram = sums[:width]
-    upper_norms = jnp.sum(sums[width : width + 8], axis=0, keepdims=True)
-    lower_norms = jnp.sum(sums[width + 8 :], axis=0, keepdims=True)
+    upper_norms, lower_norms = sums[width : width + 1], sums[width + 4 : width + 5]
     upper_norms = jnp.broadcast_to(upper_norms, (width, width)).T
     gap = upper_norms - lower_norms
     both = upper_norms + lower_norms

time: 79.1 us -> 79.1 us (level)
  the two profiles are of different devices: /device:TPU:1 before, /device:TPU:27 now
where the time goes in v4:
time: 79.1 us; the launch traced here: 78.9 us
  starting transfers between devices  29.8 us (38%)
  Pallas kernels  24.1 us (30%)
  waiting for transfers between devices  24.1 us (30%)
    ppermute x4, starting transfers between devices, from_three(): lax.ppermute(value, 'row', [r for r in row_route(**second) if r[0] % 2])  16.8 us
    pallas_call x1, Pallas kernels, rotated_last(): pl.pallas_call(functools.partial(last_kernel, row_total), out_shape=(jax....  12.9 us
    pallas_call x1, Pallas kernels, rotated(): pl.pallas_call(functools.partial(rotate_kernel, row_total), out_shape=(ja...  9.5 us
    ppermute x2, waiting for transfers between devices, from_behind(): lax.ppermute(block, 'col', [((i - distance) % devices, i) for i in range(...  8.89 us
    ppermute x4, starting transfers between devices, from_three(): added = lax.ppermute(value, 'row', route)  8.31 us
    ppermute x4, waiting for transfers between devices, from_three(): lax.ppermute(value, 'row', [r for r in row_route(**second) if r[0] % 2])  8.05 us
    ppermute x6, waiting for transfers between devices, across(): return lax.ppermute(value, 'row', row_route(**kinds))  6.46 us
    ppermute x6, starting transfers between devices, across(): return lax.ppermute(value, 'row', row_route(**kinds))  3.16 us
  transfers between devices with their start and end apart: 16, of which 13 were waited for; matrix products, arithmetic and copies ran while one was open for 0% of the time, Pallas kernels for 0%

profile of v4, /device:TPU:27, one launch (start us, length us, event | category | flops | bytes accessed | tf_op | source)
XLA Modules:
  0.0 78.9 jit_solution(17816885977723573927)
XLA Ops:
  0.6 1.4 %first_statistics.1 = f32[136,128]{1,0:T(8,128)S(1)} custom-call(f32[512,128]{1,0:T(8,128)} %upper_ref.1, f32[512,128]{1,0:T(8,128)} %lower_ref.1), custom_call_target="tpu_custom_call" | custom-call | tf_op jit(solution)/shard_map/first_statistics/pallas_call | solution.py:118
  2.1 0.8 collective-permute-start
  2.8 0.9 %collective-permute-done = f32[136,128]{1,0:T(8,128)S(1)} collective-permute-done((f32[136,128]{1,0:T(8,128)S(1)}, f32[136,128]{1,0:T(8,128)S(1)}, u32[]{:S(2)}, u32[]{:S(2)}) %collective-permute-start) | collective-permute-done | bytes 69664 | tf_op jit(solution)/shard_map/ppermute | solution.py:33
  3.8 3.1 %collective-permute-start.2 = (f32[136,128]{1,0:T(8,128)S(1)}, f32[136,128]{1,0:T(8,128)S(1)}, u32[]{:S(2)}, u32[]{:S(2)}) collective-permute-start(f32[136,128]{1,0:T(8,128)S(1)} %add.32), channel_id=1, source_target_pairs={{0,20},{2,22},{4,16},{6,18},{8,28},{10,30},{12,24},{14,26},{16,4},... | collective-permute-start | bytes 208904 | tf_op jit(solution)/shard_map/ppermute | solution.py:42
  6.8 6.1 %collective-permute-start.1 = (f32[136,128]{1,0:T(8,128)S(1)}, f32[136,128]{1,0:T(8,128)S(1)}, u32[]{:S(2)}, u32[]{:S(2)}) collective-permute-start(f32[136,128]{1,0:T(8,128)S(1)} %add.32), channel_id=1, source_target_pairs={{1,25},{3,27},{5,29},{7,31},{9,17},{11,19},{13,21},{15,23},{17,9},... | collective-permute-start | bytes 208904 | tf_op jit(solution)/shard_map/ppermute | solution.py:43
  13.0 0.0 collective-permute-done.2
  13.0 1.9 %collective-permute-done.1 = f32[136,128]{1,0:T(8,128)S(1)} collective-permute-done((f32[136,128]{1,0:T(8,128)S(1)}, f32[136,128]{1,0:T(8,128)S(1)}, u32[]{:S(2)}, u32[]{:S(2)}) %collective-permute-start.1) | collective-permute-done | bytes 69664 | tf_op jit(solution)/shard_map/ppermute | solution.py:43
  14.9 0.0 copy-start.1
  14.9 0.0 copy-start
  14.9 0.1 collective-permute-start.3
  15.0 1.2 %collective-permute-done.3 = f32[136,128]{1,0:T(8,128)S(1)} collective-permute-done((f32[136,128]{1,0:T(8,128)S(1)}, f32[136,128]{1,0:T(8,128)S(1)}, u32[]{:S(2)}, u32[]{:S(2)}) %collective-permute-start.3) | collective-permute-done | bytes 69664 | tf_op jit(solution)/shard_map/ppermute | solution.py:33
  16.3 1.9 %collective-permute-start.5 = (f32[136,128]{1,0:T(8,128)S(1)}, f32[136,128]{1,0:T(8,128)S(1)}, u32[]{:S(2)}, u32[]{:S(2)}) collective-permute-start(f32[136,128]{1,0:T(8,128)S(1)} %add.34), channel_id=1, source_target_pairs={{0,6},{2,4},{4,2},{6,0},{8,14},{10,12},{12,10},{14,8},{16,22},{18,... | collective-permute-start | bytes 208904 | tf_op jit(solution)/shard_map/ppermute | solution.py:42
  18.2 3.4 %collective-permute-start.4 = (f32[136,128]{1,0:T(8,128)S(1)}, f32[136,128]{1,0:T(8,128)S(1)}, u32[]{:S(2)}, u32[]{:S(2)}) collective-permute-start(f32[136,128]{1,0:T(8,128)S(1)} %add.34), channel_id=1, source_target_pairs={{1,5},{3,7},{5,1},{7,3},{9,13},{11,15},{13,9},{15,11},{17,21},{19,... | collective-permute-start | bytes 208904 | tf_op jit(solution)/shard_map/ppermute | solution.py:43
  21.6 0.0 collective-permute-done.5
  21.6 1.7 %collective-permute-done.4 = f32[136,128]{1,0:T(8,128)S(1)} collective-permute-done((f32[136,128]{1,0:T(8,128)S(1)}, f32[136,128]{1,0:T(8,128)S(1)}, u32[]{:S(2)}, u32[]{:S(2)}) %collective-permute-start.4) | collective-permute-done | bytes 69664 | tf_op jit(solution)/shard_map/ppermute | solution.py:43
  23.3 0.1 collective-permute-start.6
  23.4 1.2 %collective-permute-done.6.other_ref = f32[136,128]{1,0:T(8,128)S(1)} collective-permute-done((f32[136,128]{1,0:T(8,128)S(1)}, f32[136,128]{1,0:T(8,128)S(1)}, u32[]{:S(2)}, u32[]{:S(2)}) %collective-permute-start.6) | collective-permute-done | bytes 69664 | tf_op jit(solution)/shard_map/ppermute | solution.py:33
  24.7 0.0 copy-done.1
  24.7 0.0 copy-done
  24.7 9.5 %rotate.1 = (f32[512,128]{1,0:T(8,128)S(1)}, f32[512,128]{1,0:T(8,128)S(1)}) custom-call(f32[136,128]{1,0:T(8,128)S(1)} %select_add_fusion.2.mine_ref, f32[136,128]{1,0:T(8,128)S(1)} %collective-permute-done.6.other_ref, f32[512,128]{1,0:T(8,128)S(1)} %copy-done, f32[512,128]{1,0:T(8,128)S(1)} %copy-done.1), custom_call_target="tpu_custom_call" | custom-call | tf_op jit(solution)/shard_map/rotate/pallas_call | solution.py:259
  34.2 0.9 %collective-permute-start.7 = (f32[512,128]{1,0:T(8,128)S(1)}, f32[512,128]{1,0:T(8,128)S(1)}, u32[]{:S(2)}, u32[]{:S(2)}) collective-permute-start(f32[512,128]{1,0:T(8,128)S(1)} %get-tuple-element.4), channel_id=1, source_target_pairs={{224,0},{0,32},{32,64},{64,96},{96,128},{128,160},{160,192},{192,2... | collective-permute-start | bytes 786440 | tf_op jit(solution)/shard_map/ppermute | solution.py:272
  35.1 0.7 collective-permute-start.8
  35.7 6.3 %collective-permute-done.7.upper_ref = f32[512,128]{1,0:T(8,128)S(1)} collective-permute-done((f32[512,128]{1,0:T(8,128)S(1)}, f32[512,128]{1,0:T(8,128)S(1)}, u32[]{:S(2)}, u32[]{:S(2)}) %collective-permute-start.7) | collective-permute-done | bytes 262176 | tf_op jit(solution)/shard_map/ppermute | solution.py:272
  42.0 2.6 %collective-permute-done.8.lower_ref = f32[512,128]{1,0:T(8,128)S(1)} collective-permute-done((f32[512,128]{1,0:T(8,128)S(1)}, f32[512,128]{1,0:T(8,128)S(1)}, u32[]{:S(2)}, u32[]{:S(2)}) %collective-permute-start.8) | collective-permute-done | bytes 262176 | tf_op jit(solution)/shard_map/ppermute | solution.py:272
  44.6 0.3 statistics.1
  44.9 1.4 %collective-permute-start.9 = (f32[136,128]{1,0:T(8,128)S(1)}, f32[136,128]{1,0:T(8,128)S(1)}, u32[]{:S(2)}, u32[]{:S(2)}) collective-permute-start(f32[136,128]{1,0:T(8,128)S(1)} %statistics.1), channel_id=1, source_target_pairs={{0,1},{1,0},{2,3},{3,2},{4,5},{5,4},{6,7},{7,6},{8,9},{9,8},{10,11... | collective-permute-start | bytes 208904 | tf_op jit(solution)/shard_map/ppermute | solution.py:33
  46.3 0.9 %collective-permute-done.9 = f32[136,128]{1,0:T(8,128)S(1)} collective-permute-done((f32[136,128]{1,0:T(8,128)S(1)}, f32[136,128]{1,0:T(8,128)S(1)}, u32[]{:S(2)}, u32[]{:S(2)}) %collective-permute-start.9) | collective-permute-done | bytes 69664 | tf_op jit(solution)/shard_map/ppermute | solution.py:33
  47.2 2.3 %collective-permute-start.11 = (f32[136,128]{1,0:T(8,128)S(1)}, f32[136,128]{1,0:T(8,128)S(1)}, u32[]{:S(2)}, u32[]{:S(2)}) collective-permute-start(f32[136,128]{1,0:T(8,128)S(1)} %add.36), channel_id=1, source_target_pairs={{0,20},{2,22},{4,16},{6,18},{8,28},{10,30},{12,24},{14,26},{16,4},... | collective-permute-start | bytes 208904 | tf_op jit(solution)/shard_map/ppermute | solution.py:42
  49.5 4.2 %collective-permute-start.10 = (f32[136,128]{1,0:T(8,128)S(1)}, f32[136,128]{1,0:T(8,128)S(1)}, u32[]{:S(2)}, u32[]{:S(2)}) collective-permute-start(f32[136,128]{1,0:T(8,128)S(1)} %add.36), channel_id=1, source_target_pairs={{1,25},{3,27},{5,29},{7,31},{9,17},{11,19},{13,21},{15,23},{17,9},... | collective-permute-start | bytes 208904 | tf_op jit(solution)/shard_map/ppermute | solution.py:43
  53.8 0.0 collective-permute-done.11
  53.8 2.9 %collective-permute-done.10 = f32[136,128]{1,0:T(8,128)S(1)} collective-permute-done((f32[136,128]{1,0:T(8,128)S(1)}, f32[136,128]{1,0:T(8,128)S(1)}, u32[]{:S(2)}, u32[]{:S(2)}) %collective-permute-start.10) | collective-permute-done | bytes 69664 | tf_op jit(solution)/shard_map/ppermute | solution.py:43
  56.7 0.1 collective-permute-start.12
  56.8 1.2 %collective-permute-done.12 = f32[136,128]{1,0:T(8,128)S(1)} collective-permute-done((f32[136,128]{1,0:T(8,128)S(1)}, f32[136,128]{1,0:T(8,128)S(1)}, u32[]{:S(2)}, u32[]{:S(2)}) %collective-permute-start.12) | collective-permute-done | bytes 69664 | tf_op jit(solution)/shard_map/ppermute | solution.py:33
  58.1 1.0 %collective-permute-start.14 = (f32[136,128]{1,0:T(8,128)S(1)}, f32[136,128]{1,0:T(8,128)S(1)}, u32[]{:S(2)}, u32[]{:S(2)}) collective-permute-start(f32[136,128]{1,0:T(8,128)S(1)} %add.38), channel_id=1, source_target_pairs={{0,6},{2,4},{4,2},{6,0},{8,14},{10,12},{12,10},{14,8},{16,22},{18,... | collective-permute-start | bytes 208904 | tf_op jit(solution)/shard_map/ppermute | solution.py:42
  59.0 3.1 %collective-permute-start.13 = (f32[136,128]{1,0:T(8,128)S(1)}, f32[136,128]{1,0:T(8,128)S(1)}, u32[]{:S(2)}, u32[]{:S(2)}) collective-permute-start(f32[136,128]{1,0:T(8,128)S(1)} %add.38), channel_id=1, source_target_pairs={{1,5},{3,7},{5,1},{7,3},{9,13},{11,15},{13,9},{15,11},{17,21},{19,... | collective-permute-start | bytes 208904 | tf_op jit(solution)/shard_map/ppermute | solution.py:43
  62.1 0.7 collective-permute-done.14
  62.8 1.6 %collective-permute-done.13 = f32[136,128]{1,0:T(8,128)S(1)} collective-permute-done((f32[136,128]{1,0:T(8,128)S(1)}, f32[136,128]{1,0:T(8,128)S(1)}, u32[]{:S(2)}, u32[]{:S(2)}) %collective-permute-start.13) | collective-permute-done | bytes 69664 | tf_op jit(solution)/shard_map/ppermute | solution.py:43
  64.4 0.7 collective-permute-start.15
  65.1 0.9 %collective-permute-done.15.other_ref = f32[136,128]{1,0:T(8,128)S(1)} collective-permute-done((f32[136,128]{1,0:T(8,128)S(1)}, f32[136,128]{1,0:T(8,128)S(1)}, u32[]{:S(2)}, u32[]{:S(2)}) %collective-permute-start.15) | collective-permute-done | bytes 69664 | tf_op jit(solution)/shard_map/ppermute | solution.py:33
  66.0 12.9 %rotate_last.1 = (f32[512,128]{1,0:T(8,128)}, f32[512,128]{1,0:T(8,128)}) custom-call(f32[136,128]{1,0:T(8,128)S(1)} %select_add_fusion.mine_ref, f32[136,128]{1,0:T(8,128)S(1)} %collective-permute-done.15.other_ref, f32[512,128]{1,0:T(8,128)S(1)} %collective-permute-done.7.upper_ref, f32[512,128]{1,0:T(8,128)S(1)} %collective-permute-done.8.lower_ref), custom_call_target="tpu_custom_call" | custom-call | tf_op jit(solution)/shard_map/rotate_last/pallas_call | solution.py:235
  (8 shorter events, 0.1 us)
Async XLA Ops:
  2.1 1.7 %collective-permute-start = (f32[136,128]{1,0:T(8,128)S(1)}, f32[136,128]{1,0:T(8,128)S(1)}, u32[]{:S(2)}, u32[]{:S(2)}) collective-permute-start(f32[136,128]{1,0:T(8,128)S(1)} %first_statistics.1), channel_id=1, source_target_pairs={{0,1},{1,0},{2,3},{3,2},{4,5},{5,4},{6,7},{7,6},{8,9},{9,8},{10,11... | collective-permute-start | bytes 208904 | tf_op jit(solution)/shard_map/ppermute | solution.py:33
  3.8 9.2 %collective-permute-start.2 = (f32[136,128]{1,0:T(8,128)S(1)}, f32[136,128]{1,0:T(8,128)S(1)}, u32[]{:S(2)}, u32[]{:S(2)}) collective-permute-start(f32[136,128]{1,0:T(8,128)S(1)} %add.32), channel_id=1, source_target_pairs={{0,20},{2,22},{4,16},{6,18},{8,28},{10,30},{12,24},{14,26},{16,4},... | collective-permute-start | bytes 208904 | tf_op jit(solution)/shard_map/ppermute | solution.py:42
  6.8 8.0 %collective-permute-start.1 = (f32[136,128]{1,0:T(8,128)S(1)}, f32[136,128]{1,0:T(8,128)S(1)}, u32[]{:S(2)}, u32[]{:S(2)}) collective-permute-start(f32[136,128]{1,0:T(8,128)S(1)} %add.32), channel_id=1, source_target_pairs={{1,25},{3,27},{5,29},{7,31},{9,17},{11,19},{13,21},{15,23},{17,9},... | collective-permute-start | bytes 208904 | tf_op jit(solution)/shard_map/ppermute | solution.py:43
  14.9 9.8 %copy-start.1 = (f32[512,128]{1,0:T(8,128)S(1)}, f32[512,128]{1,0:T(8,128)}, u32[]{:S(2)}) copy-start(f32[512,128]{1,0:T(8,128)} %lower_ref.1) | copy-start | bytes 786436
  14.9 9.7 %copy-start = (f32[512,128]{1,0:T(8,128)S(1)}, f32[512,128]{1,0:T(8,128)}, u32[]{:S(2)}) copy-start(f32[512,128]{1,0:T(8,128)} %upper_ref.1) | copy-start | bytes 786436
  14.9 1.3 %collective-permute-start.3 = (f32[136,128]{1,0:T(8,128)S(1)}, f32[136,128]{1,0:T(8,128)S(1)}, u32[]{:S(2)}, u32[]{:S(2)}) collective-permute-start(f32[136,128]{1,0:T(8,128)S(1)} %select_add_fusion.3), channel_id=1, source_target_pairs={{0,1},{1,0},{2,3},{3,2},{4,5},{5,4},{6,7},{7,6},{8,9},{9,8},{10,11... | collective-permute-start | bytes 208904 | tf_op jit(solution)/shard_map/ppermute | solution.py:33
  16.3 5.3 %collective-permute-start.5 = (f32[136,128]{1,0:T(8,128)S(1)}, f32[136,128]{1,0:T(8,128)S(1)}, u32[]{:S(2)}, u32[]{:S(2)}) collective-permute-start(f32[136,128]{1,0:T(8,128)S(1)} %add.34), channel_id=1, source_target_pairs={{0,6},{2,4},{4,2},{6,0},{8,14},{10,12},{12,10},{14,8},{16,22},{18,... | collective-permute-start | bytes 208904 | tf_op jit(solution)/shard_map/ppermute | solution.py:42
  18.2 5.1 %collective-permute-start.4 = (f32[136,128]{1,0:T(8,128)S(1)}, f32[136,128]{1,0:T(8,128)S(1)}, u32[]{:S(2)}, u32[]{:S(2)}) collective-permute-start(f32[136,128]{1,0:T(8,128)S(1)} %add.34), channel_id=1, source_target_pairs={{1,5},{3,7},{5,1},{7,3},{9,13},{11,15},{13,9},{15,11},{17,21},{19,... | collective-permute-start | bytes 208904 | tf_op jit(solution)/shard_map/ppermute | solution.py:43
  23.3 1.3 %collective-permute-start.6 = (f32[136,128]{1,0:T(8,128)S(1)}, f32[136,128]{1,0:T(8,128)S(1)}, u32[]{:S(2)}, u32[]{:S(2)}) collective-permute-start(f32[136,128]{1,0:T(8,128)S(1)} %select_add_fusion.2.mine_ref), channel_id=1, source_target_pairs={{0,1},{1,0},{2,3},{3,2},{4,5},{5,4},{6,7},{7,6},{8,9},{9,8},{10,11... | collective-permute-start | bytes 208904 | tf_op jit(solution)/shard_map/ppermute | solution.py:33
  34.2 7.8 %collective-permute-start.7 = (f32[512,128]{1,0:T(8,128)S(1)}, f32[512,128]{1,0:T(8,128)S(1)}, u32[]{:S(2)}, u32[]{:S(2)}) collective-permute-start(f32[512,128]{1,0:T(8,128)S(1)} %get-tuple-element.4), channel_id=1, source_target_pairs={{224,0},{0,32},{32,64},{64,96},{96,128},{128,160},{160,192},{192,2... | collective-permute-start | bytes 786440 | tf_op jit(solution)/shard_map/ppermute | solution.py:272
  35.1 9.5 %collective-permute-start.8 = (f32[512,128]{1,0:T(8,128)S(1)}, f32[512,128]{1,0:T(8,128)S(1)}, u32[]{:S(2)}, u32[]{:S(2)}) collective-permute-start(f32[512,128]{1,0:T(8,128)S(1)} %get-tuple-element.5), channel_id=1, source_target_pairs={{32,0},{64,32},{96,64},{128,96},{160,128},{192,160},{224,192},{0,2... | collective-permute-start | bytes 786440 | tf_op jit(solution)/shard_map/ppermute | solution.py:272
  44.9 2.3 %collective-permute-start.9 = (f32[136,128]{1,0:T(8,128)S(1)}, f32[136,128]{1,0:T(8,128)S(1)}, u32[]{:S(2)}, u32[]{:S(2)}) collective-permute-start(f32[136,128]{1,0:T(8,128)S(1)} %statistics.1), channel_id=1, source_target_pairs={{0,1},{1,0},{2,3},{3,2},{4,5},{5,4},{6,7},{7,6},{8,9},{9,8},{10,11... | collective-permute-start | bytes 208904 | tf_op jit(solution)/shard_map/ppermute | solution.py:33
  47.2 6.6 %collective-permute-start.11 = (f32[136,128]{1,0:T(8,128)S(1)}, f32[136,128]{1,0:T(8,128)S(1)}, u32[]{:S(2)}, u32[]{:S(2)}) collective-permute-start(f32[136,128]{1,0:T(8,128)S(1)} %add.36), channel_id=1, source_target_pairs={{0,20},{2,22},{4,16},{6,18},{8,28},{10,30},{12,24},{14,26},{16,4},... | collective-permute-start | bytes 208904 | tf_op jit(solution)/shard_map/ppermute | solution.py:42
  49.5 7.2 %collective-permute-start.10 = (f32[136,128]{1,0:T(8,128)S(1)}, f32[136,128]{1,0:T(8,128)S(1)}, u32[]{:S(2)}, u32[]{:S(2)}) collective-permute-start(f32[136,128]{1,0:T(8,128)S(1)} %add.36), channel_id=1, source_target_pairs={{1,25},{3,27},{5,29},{7,31},{9,17},{11,19},{13,21},{15,23},{17,9},... | collective-permute-start | bytes 208904 | tf_op jit(solution)/shard_map/ppermute | solution.py:43
  56.7 1.3 %collective-permute-start.12 = (f32[136,128]{1,0:T(8,128)S(1)}, f32[136,128]{1,0:T(8,128)S(1)}, u32[]{:S(2)}, u32[]{:S(2)}) collective-permute-start(f32[136,128]{1,0:T(8,128)S(1)} %select_add_fusion.1), channel_id=1, source_target_pairs={{0,1},{1,0},{2,3},{3,2},{4,5},{5,4},{6,7},{7,6},{8,9},{9,8},{10,11... | collective-permute-start | bytes 208904 | tf_op jit(solution)/shard_map/ppermute | solution.py:33
  58.1 4.8 %collective-permute-start.14 = (f32[136,128]{1,0:T(8,128)S(1)}, f32[136,128]{1,0:T(8,128)S(1)}, u32[]{:S(2)}, u32[]{:S(2)}) collective-permute-start(f32[136,128]{1,0:T(8,128)S(1)} %add.38), channel_id=1, source_target_pairs={{0,6},{2,4},{4,2},{6,0},{8,14},{10,12},{12,10},{14,8},{16,22},{18,... | collective-permute-start | bytes 208904 | tf_op jit(solution)/shard_map/ppermute | solution.py:42
  59.0 5.3 %collective-permute-start.13 = (f32[136,128]{1,0:T(8,128)S(1)}, f32[136,128]{1,0:T(8,128)S(1)}, u32[]{:S(2)}, u32[]{:S(2)}) collective-permute-start(f32[136,128]{1,0:T(8,128)S(1)} %add.38), channel_id=1, source_target_pairs={{1,5},{3,7},{5,1},{7,3},{9,13},{11,15},{13,9},{15,11},{17,21},{19,... | collective-permute-start | bytes 208904 | tf_op jit(solution)/shard_map/ppermute | solution.py:43
  64.4 1.6 %collective-permute-start.15 = (f32[136,128]{1,0:T(8,128)S(1)}, f32[136,128]{1,0:T(8,128)S(1)}, u32[]{:S(2)}, u32[]{:S(2)}) collective-permute-start(f32[136,128]{1,0:T(8,128)S(1)} %select_add_fusion.mine_ref), channel_id=1, source_target_pairs={{0,1},{1,0},{2,3},{3,2},{4,5},{5,4},{6,7},{7,6},{8,9},{9,8},{10,11... | collective-permute-start | bytes 208904 | tf_op jit(solution)/shard_map/ppermute | solution.py:33

commit v5 on v4

--- a/solution.py
+++ b/solution.py
@@ -152,7 +152,7 @@
     return -cross_gram * gap / (2.0 * gap * gap + 0.5 * both * both + 1e-05)
 
 
-def solved(coupling, residual_ref, result_ref):
+def scaled_residual(coupling):
     width = coupling.shape[0]
     identity = (
         lax.broadcasted_iota(jnp.int32, (width, width), 0) == lax.broadcasted_iota(jnp.int32, (width, width), 1)
@@ -161,15 +161,19 @@
     outer = contract(parts, parts, ((1,), (1,)))
     size = jnp.sqrt(jnp.sum(jnp.sum(outer * outer, axis=0, keepdims=True), axis=1, keepdims=True))
     alpha = 2.0 / (2.0 + size)
-    bound = jnp.sum(size / (2.0 + size))
-    residual = (1.0 - alpha) * identity - alpha * outer
-
+    return (1.0 - alpha) * identity - alpha * outer, alpha, jnp.sum(size / (2.0 + size))
+
+
+def two_factors(residual, right):
+    parts = split(residual)
+    right = right + contract(parts, split(right), ((1,), (0,)))
+    square = contract(parts, parts, ((1,), (0,)))
+    return right + contract(split(square), split(right), ((1,), (0,))), square
+
+
+def solved(coupling, residual, alpha, bound, residual_ref, result_ref):
     def series(right):
-        parts = split(residual)
-        right = right + contract(parts, split(right), ((1,), (0,)))
-        square = contract(parts, parts, ((1,), (0,)))
-        residual_ref[...] = square
-        result_ref[...] = right + contract(split(square), split(right), ((1,), (0,)))
+        result_ref[...], residual_ref[...] = two_factors(residual, right)
 
         def factor(bound):
             square = exact_dot(residual_ref[...], residual_ref[...])
@@ -190,6 +194,16 @@
             result_ref[...] += value
 
     return result_ref[...]
+
+
+def with_rotation(sums, row_total, scratch, use):
+    coupling = coupling_of(sums, row_total)
+    residual, alpha, bound = scaled_residual(coupling)
+    use(full_change(coupling, two_factors(residual, (2.0 * alpha) * coupling)[0]))
+
+    @pl.when((bound * bound) * (bound * bound) > TOLERANCE)
+    def _():
+        use(full_change(coupling, solved(coupling, residual, alpha, bound, *scratch)))
 
 
 def apply(upper, lower, change):
@@ -213,20 +227,21 @@
 
 def last_kernel(row_total, mine_ref, other_ref, upper_ref, lower_ref, upper_hbm, lower_hbm, residual_ref, result_ref,
                 new_upper_ref, new_lower_ref, sems):
-    coupling = coupling_of(mine_ref[...] + other_ref[...], row_total)
-    to_lower = solved(coupling, residual_ref, result_ref)
-    change = full_change(coupling, to_lower)
     width = upper_ref.shape[1]
-    copies = []
-    for j, rows in enumerate(pieces_of(upper_ref.shape[0])):
-        moved = apply(upper_ref[rows], lower_ref[rows], change)
-        new_upper_ref[rows] = upper_ref[rows] + moved[:, :width]
-        new_lower_ref[rows] = lower_ref[rows] + moved[:, width:]
-        for i, (source, target) in enumerate(((new_upper_ref, upper_hbm), (new_lower_ref, lower_hbm))):
-            copies.append(pltpu.make_async_copy(source.at[rows], target.at[rows], sems.at[i, j]))
-            copies[-1].start()
-    for copy in copies:
-        copy.wait()
+
+    def use(change):
+        copies = []
+        for j, rows in enumerate(pieces_of(upper_ref.shape[0])):
+            moved = apply(upper_ref[rows], lower_ref[rows], change)
+            new_upper_ref[rows] = upper_ref[rows] + moved[:, :width]
+            new_lower_ref[rows] = lower_ref[rows] + moved[:, width:]
+            for i, (source, target) in enumerate(((new_upper_ref, upper_hbm), (new_lower_ref, lower_hbm))):
+                copies.append(pltpu.make_async_copy(source.at[rows], target.at[rows], sems.at[i, j]))
+                copies[-1].start()
+        for copy in copies:
+            copy.wait()
+
+    with_rotation(mine_ref[...] + other_ref[...], row_total, (residual_ref, result_ref), use)
 
 
 def rotated_last(mine, other, upper, lower, row_total):
@@ -246,12 +261,14 @@
 
 
 def rotate_kernel(row_total, mine_ref, other_ref, upper_ref, lower_ref, new_upper_ref, new_lower_ref, residual_ref, result_ref):
-    coupling = coupling_of(mine_ref[...] + other_ref[...], row_total)
-    to_lower = solved(coupling, residual_ref, result_ref)
     width = upper_ref.shape[1]
-    moved = apply(upper_ref[...], lower_ref[...], full_change(coupling, to_lower))
-    new_upper_ref[...] = upper_ref[...] + moved[:, :width]
-    new_lower_ref[...] = lower_ref[...] + moved[:, width:]
+
+    def use(change):
+        moved = apply(upper_ref[...], lower_ref[...], change)
+        new_upper_ref[...] = upper_ref[...] + moved[:, :width]
+        new_lower_ref[...] = lower_ref[...] + moved[:, width:]
+
+    with_rotation(mine_ref[...] + other_ref[...], row_total, (residual_ref, result_ref), use)
 
 
 def rotated(mine, other, upper, lower, row_total):

time: 79.1 us -> 80 us (1.011)
  the two profiles are of different devices: /device:TPU:27 before, /device:TPU:25 now
where the time goes in v5:
time: 80 us; the launch traced here: 80.3 us
  starting transfers between devices  31 us (39%)
  Pallas kernels  24.8 us (31%)
  waiting for transfers between devices  23.6 us (30%)
  between operations  0.8 us (1%)
    ppermute x4, starting transfers between devices, from_three(): lax.ppermute(value, 'row', [r for r in row_route(**second) if r[0] % 2])  16.8 us
    pallas_call x1, Pallas kernels, rotated_last(): pl.pallas_call(functools.partial(last_kernel, row_total), out_shape=(jax....  12.9 us
    ppermute x4, starting transfers between devices, from_three(): added = lax.ppermute(value, 'row', route)  10.3 us
    pallas_call x1, Pallas kernels, rotated(): pl.pallas_call(functools.partial(rotate_kernel, row_total), out_shape=(ja...  10.1 us
    ppermute x4, waiting for transfers between devices, from_three(): lax.ppermute(value, 'row', [r for r in row_route(**second) if r[0] % 2])  8.45 us
    ppermute x2, waiting for transfers between devices, from_behind(): lax.ppermute(block, 'col', [((i - distance) % devices, i) for i in range(...  8.3 us
    ppermute x6, waiting for transfers between devices, across(): return lax.ppermute(value, 'row', row_route(**kinds))  6.8 us
    ppermute x6, starting transfers between devices, across(): return lax.ppermute(value, 'row', row_route(**kinds))  2.37 us
  transfers between devices with their start and end apart: 16, of which 12 were waited for; matrix products, arithmetic and copies ran while one was open for 0% of the time, Pallas kernels for 0%

profile of v5, /device:TPU:25, one launch (start us, length us, event | category | flops | bytes accessed | tf_op | source)
XLA Modules:
  0.0 80.3 jit_solution(13625584295498526046)
XLA Ops:
  0.6 1.4 %first_statistics.1 = f32[136,128]{1,0:T(8,128)S(1)} custom-call(f32[512,128]{1,0:T(8,128)} %upper_ref.1, f32[512,128]{1,0:T(8,128)} %lower_ref.1), custom_call_target="tpu_custom_call" | custom-call | tf_op jit(solution)/shard_map/first_statistics/pallas_call | solution.py:118
  2.1 0.8 collective-permute-start
  2.8 0.9 %collective-permute-done = f32[136,128]{1,0:T(8,128)S(1)} collective-permute-done((f32[136,128]{1,0:T(8,128)S(1)}, f32[136,128]{1,0:T(8,128)S(1)}, u32[]{:S(2)}, u32[]{:S(2)}) %collective-permute-start) | collective-permute-done | bytes 69664 | tf_op jit(solution)/shard_map/ppermute | solution.py:33
  3.8 3.1 %collective-permute-start.2 = (f32[136,128]{1,0:T(8,128)S(1)}, f32[136,128]{1,0:T(8,128)S(1)}, u32[]{:S(2)}, u32[]{:S(2)}) collective-permute-start(f32[136,128]{1,0:T(8,128)S(1)} %add.32), channel_id=1, source_target_pairs={{0,20},{2,22},{4,16},{6,18},{8,28},{10,30},{12,24},{14,26},{16,4},... | collective-permute-start | bytes 208904 | tf_op jit(solution)/shard_map/ppermute | solution.py:42
  6.8 6.1 %collective-permute-start.1 = (f32[136,128]{1,0:T(8,128)S(1)}, f32[136,128]{1,0:T(8,128)S(1)}, u32[]{:S(2)}, u32[]{:S(2)}) collective-permute-start(f32[136,128]{1,0:T(8,128)S(1)} %add.32), channel_id=1, source_target_pairs={{1,25},{3,27},{5,29},{7,31},{9,17},{11,19},{13,21},{15,23},{17,9},... | collective-permute-start | bytes 208904 | tf_op jit(solution)/shard_map/ppermute | solution.py:43
  13.0 0.0 collective-permute-done.2
  13.0 1.9 %collective-permute-done.1 = f32[136,128]{1,0:T(8,128)S(1)} collective-permute-done((f32[136,128]{1,0:T(8,128)S(1)}, f32[136,128]{1,0:T(8,128)S(1)}, u32[]{:S(2)}, u32[]{:S(2)}) %collective-permute-start.1) | collective-permute-done | bytes 69664 | tf_op jit(solution)/shard_map/ppermute | solution.py:43
  14.9 0.0 copy-start.1
  14.9 0.0 copy-start
  14.9 0.1 collective-permute-start.3
  15.0 1.2 %collective-permute-done.3 = f32[136,128]{1,0:T(8,128)S(1)} collective-permute-done((f32[136,128]{1,0:T(8,128)S(1)}, f32[136,128]{1,0:T(8,128)S(1)}, u32[]{:S(2)}, u32[]{:S(2)}) %collective-permute-start.3) | collective-permute-done | bytes 69664 | tf_op jit(solution)/shard_map/ppermute | solution.py:33
  16.3 2.8 %collective-permute-start.5 = (f32[136,128]{1,0:T(8,128)S(1)}, f32[136,128]{1,0:T(8,128)S(1)}, u32[]{:S(2)}, u32[]{:S(2)}) collective-permute-start(f32[136,128]{1,0:T(8,128)S(1)} %add.34), channel_id=1, source_target_pairs={{0,6},{2,4},{4,2},{6,0},{8,14},{10,12},{12,10},{14,8},{16,22},{18,... | collective-permute-start | bytes 208904 | tf_op jit(solution)/shard_map/ppermute | solution.py:42
  19.1 3.4 %collective-permute-start.4 = (f32[136,128]{1,0:T(8,128)S(1)}, f32[136,128]{1,0:T(8,128)S(1)}, u32[]{:S(2)}, u32[]{:S(2)}) collective-permute-start(f32[136,128]{1,0:T(8,128)S(1)} %add.34), channel_id=1, source_target_pairs={{1,5},{3,7},{5,1},{7,3},{9,13},{11,15},{13,9},{15,11},{17,21},{19,... | collective-permute-start | bytes 208904 | tf_op jit(solution)/shard_map/ppermute | solution.py:43
  22.5 0.0 collective-permute-done.5
  22.5 1.7 %collective-permute-done.4 = f32[136,128]{1,0:T(8,128)S(1)} collective-permute-done((f32[136,128]{1,0:T(8,128)S(1)}, f32[136,128]{1,0:T(8,128)S(1)}, u32[]{:S(2)}, u32[]{:S(2)}) %collective-permute-start.4) | collective-permute-done | bytes 69664 | tf_op jit(solution)/shard_map/ppermute | solution.py:43
  24.2 0.1 collective-permute-start.6
  24.3 1.2 %collective-permute-done.6.other_ref = f32[136,128]{1,0:T(8,128)S(1)} collective-permute-done((f32[136,128]{1,0:T(8,128)S(1)}, f32[136,128]{1,0:T(8,128)S(1)}, u32[]{:S(2)}, u32[]{:S(2)}) %collective-permute-start.6) | collective-permute-done | bytes 69664 | tf_op jit(solution)/shard_map/ppermute | solution.py:33
  25.5 0.0 copy-done.1
  25.6 0.0 copy-done
  25.6 10.1 %rotate.1 = (f32[512,128]{1,0:T(8,128)S(1)}, f32[512,128]{1,0:T(8,128)S(1)}) custom-call(f32[136,128]{1,0:T(8,128)S(1)} %select_add_fusion.2.mine_ref, f32[136,128]{1,0:T(8,128)S(1)} %collective-permute-done.6.other_ref, f32[512,128]{1,0:T(8,128)S(1)} %copy-done, f32[512,128]{1,0:T(8,128)S(1)} %copy-done.1), custom_call_target="tpu_custom_call" | custom-call | tf_op jit(solution)/shard_map/rotate/pallas_call | solution.py:276
  35.7 0.1 collective-permute-start.7
  35.8 1.5 %collective-permute-start.8 = (f32[512,128]{1,0:T(8,128)S(1)}, f32[512,128]{1,0:T(8,128)S(1)}, u32[]{:S(2)}, u32[]{:S(2)}) collective-permute-start(f32[512,128]{1,0:T(8,128)S(1)} %get-tuple-element.5), channel_id=1, source_target_pairs={{32,0},{64,32},{96,64},{128,96},{160,128},{192,160},{224,192},{0,2... | collective-permute-start | bytes 786440 | tf_op jit(solution)/shard_map/ppermute | solution.py:289
  37.2 6.3 %collective-permute-done.7.upper_ref = f32[512,128]{1,0:T(8,128)S(1)} collective-permute-done((f32[512,128]{1,0:T(8,128)S(1)}, f32[512,128]{1,0:T(8,128)S(1)}, u32[]{:S(2)}, u32[]{:S(2)}) %collective-permute-start.7) | collective-permute-done | bytes 262176 | tf_op jit(solution)/shard_map/ppermute | solution.py:289
  43.5 2.0 %collective-permute-done.8.lower_ref = f32[512,128]{1,0:T(8,128)S(1)} collective-permute-done((f32[512,128]{1,0:T(8,128)S(1)}, f32[512,128]{1,0:T(8,128)S(1)}, u32[]{:S(2)}, u32[]{:S(2)}) %collective-permute-start.8) | collective-permute-done | bytes 262176 | tf_op jit(solution)/shard_map/ppermute | solution.py:289
  45.5 0.3 statistics.1
  45.9 1.2 %collective-permute-start.9 = (f32[136,128]{1,0:T(8,128)S(1)}, f32[136,128]{1,0:T(8,128)S(1)}, u32[]{:S(2)}, u32[]{:S(2)}) collective-permute-start(f32[136,128]{1,0:T(8,128)S(1)} %statistics.1), channel_id=1, source_target_pairs={{0,1},{1,0},{2,3},{3,2},{4,5},{5,4},{6,7},{7,6},{8,9},{9,8},{10,11... | collective-permute-start | bytes 208904 | tf_op jit(solution)/shard_map/ppermute | solution.py:33
  47.1 0.9 %collective-permute-done.9 = f32[136,128]{1,0:T(8,128)S(1)} collective-permute-done((f32[136,128]{1,0:T(8,128)S(1)}, f32[136,128]{1,0:T(8,128)S(1)}, u32[]{:S(2)}, u32[]{:S(2)}) %collective-permute-start.9) | collective-permute-done | bytes 69664 | tf_op jit(solution)/shard_map/ppermute | solution.py:33
  48.0 2.3 %collective-permute-start.11 = (f32[136,128]{1,0:T(8,128)S(1)}, f32[136,128]{1,0:T(8,128)S(1)}, u32[]{:S(2)}, u32[]{:S(2)}) collective-permute-start(f32[136,128]{1,0:T(8,128)S(1)} %add.36), channel_id=1, source_target_pairs={{0,20},{2,22},{4,16},{6,18},{8,28},{10,30},{12,24},{14,26},{16,4},... | collective-permute-start | bytes 208904 | tf_op jit(solution)/shard_map/ppermute | solution.py:42
  50.4 4.2 %collective-permute-start.10 = (f32[136,128]{1,0:T(8,128)S(1)}, f32[136,128]{1,0:T(8,128)S(1)}, u32[]{:S(2)}, u32[]{:S(2)}) collective-permute-start(f32[136,128]{1,0:T(8,128)S(1)} %add.36), channel_id=1, source_target_pairs={{1,25},{3,27},{5,29},{7,31},{9,17},{11,19},{13,21},{15,23},{17,9},... | collective-permute-start | bytes 208904 | tf_op jit(solution)/shard_map/ppermute | solution.py:43
  54.6 0.0 collective-permute-done.11
  54.6 2.9 %collective-permute-done.10 = f32[136,128]{1,0:T(8,128)S(1)} collective-permute-done((f32[136,128]{1,0:T(8,128)S(1)}, f32[136,128]{1,0:T(8,128)S(1)}, u32[]{:S(2)}, u32[]{:S(2)}) %collective-permute-start.10) | collective-permute-done | bytes 69664 | tf_op jit(solution)/shard_map/ppermute | solution.py:43
  57.5 0.1 collective-permute-start.12
  57.6 1.2 %collective-permute-done.12 = f32[136,128]{1,0:T(8,128)S(1)} collective-permute-done((f32[136,128]{1,0:T(8,128)S(1)}, f32[136,128]{1,0:T(8,128)S(1)}, u32[]{:S(2)}, u32[]{:S(2)}) %collective-permute-start.12) | collective-permute-done | bytes 69664 | tf_op jit(solution)/shard_map/ppermute | solution.py:33
  58.9 2.0 %collective-permute-start.14 = (f32[136,128]{1,0:T(8,128)S(1)}, f32[136,128]{1,0:T(8,128)S(1)}, u32[]{:S(2)}, u32[]{:S(2)}) collective-permute-start(f32[136,128]{1,0:T(8,128)S(1)} %add.38), channel_id=1, source_target_pairs={{0,6},{2,4},{4,2},{6,0},{8,14},{10,12},{12,10},{14,8},{16,22},{18,... | collective-permute-start | bytes 208904 | tf_op jit(solution)/shard_map/ppermute | solution.py:42
  60.9 3.1 %collective-permute-start.13 = (f32[136,128]{1,0:T(8,128)S(1)}, f32[136,128]{1,0:T(8,128)S(1)}, u32[]{:S(2)}, u32[]{:S(2)}) collective-permute-start(f32[136,128]{1,0:T(8,128)S(1)} %add.38), channel_id=1, source_target_pairs={{1,5},{3,7},{5,1},{7,3},{9,13},{11,15},{13,9},{15,11},{17,21},{19,... | collective-permute-start | bytes 208904 | tf_op jit(solution)/shard_map/ppermute | solution.py:43
  64.0 0.0 collective-permute-done.14
  64.1 1.9 %collective-permute-done.13 = f32[136,128]{1,0:T(8,128)S(1)} collective-permute-done((f32[136,128]{1,0:T(8,128)S(1)}, f32[136,128]{1,0:T(8,128)S(1)}, u32[]{:S(2)}, u32[]{:S(2)}) %collective-permute-start.13) | collective-permute-done | bytes 69664 | tf_op jit(solution)/shard_map/ppermute | solution.py:43
  66.0 0.1 collective-permute-start.15
  66.1 1.2 %collective-permute-done.15.other_ref = f32[136,128]{1,0:T(8,128)S(1)} collective-permute-done((f32[136,128]{1,0:T(8,128)S(1)}, f32[136,128]{1,0:T(8,128)S(1)}, u32[]{:S(2)}, u32[]{:S(2)}) %collective-permute-start.15) | collective-permute-done | bytes 69664 | tf_op jit(solution)/shard_map/ppermute | solution.py:33
  67.3 12.9 %rotate_last.1 = (f32[512,128]{1,0:T(8,128)}, f32[512,128]{1,0:T(8,128)}) custom-call(f32[136,128]{1,0:T(8,128)S(1)} %select_add_fusion.mine_ref, f32[136,128]{1,0:T(8,128)S(1)} %collective-permute-done.15.other_ref, f32[512,128]{1,0:T(8,128)S(1)} %collective-permute-done.7.upper_ref, f32[512,128]{1,0:T(8,128)S(1)} %collective-permute-done.8.lower_ref), custom_call_target="tpu_custom_call" | custom-call | tf_op jit(solution)/shard_map/rotate_last/pallas_call | solution.py:250
  (8 shorter events, 0.1 us)
Async XLA Ops:
  2.1 1.7 %collective-permute-start = (f32[136,128]{1,0:T(8,128)S(1)}, f32[136,128]{1,0:T(8,128)S(1)}, u32[]{:S(2)}, u32[]{:S(2)}) collective-permute-start(f32[136,128]{1,0:T(8,128)S(1)} %first_statistics.1), channel_id=1, source_target_pairs={{0,1},{1,0},{2,3},{3,2},{4,5},{5,4},{6,7},{7,6},{8,9},{9,8},{10,11... | collective-permute-start | bytes 208904 | tf_op jit(solution)/shard_map/ppermute | solution.py:33
  3.8 9.2 %collective-permute-start.2 = (f32[136,128]{1,0:T(8,128)S(1)}, f32[136,128]{1,0:T(8,128)S(1)}, u32[]{:S(2)}, u32[]{:S(2)}) collective-permute-start(f32[136,128]{1,0:T(8,128)S(1)} %add.32), channel_id=1, source_target_pairs={{0,20},{2,22},{4,16},{6,18},{8,28},{10,30},{12,24},{14,26},{16,4},... | collective-permute-start | bytes 208904 | tf_op jit(solution)/shard_map/ppermute | solution.py:42
  6.8 8.0 %collective-permute-start.1 = (f32[136,128]{1,0:T(8,128)S(1)}, f32[136,128]{1,0:T(8,128)S(1)}, u32[]{:S(2)}, u32[]{:S(2)}) collective-permute-start(f32[136,128]{1,0:T(8,128)S(1)} %add.32), channel_id=1, source_target_pairs={{1,25},{3,27},{5,29},{7,31},{9,17},{11,19},{13,21},{15,23},{17,9},... | collective-permute-start | bytes 208904 | tf_op jit(solution)/shard_map/ppermute | solution.py:43
  14.9 10.7 %copy-start.1 = (f32[512,128]{1,0:T(8,128)S(1)}, f32[512,128]{1,0:T(8,128)}, u32[]{:S(2)}) copy-start(f32[512,128]{1,0:T(8,128)} %lower_ref.1) | copy-start | bytes 786436
  14.9 10.6 %copy-start = (f32[512,128]{1,0:T(8,128)S(1)}, f32[512,128]{1,0:T(8,128)}, u32[]{:S(2)}) copy-start(f32[512,128]{1,0:T(8,128)} %upper_ref.1) | copy-start | bytes 786436
  14.9 1.3 %collective-permute-start.3 = (f32[136,128]{1,0:T(8,128)S(1)}, f32[136,128]{1,0:T(8,128)S(1)}, u32[]{:S(2)}, u32[]{:S(2)}) collective-permute-start(f32[136,128]{1,0:T(8,128)S(1)} %select_add_fusion.3), channel_id=1, source_target_pairs={{0,1},{1,0},{2,3},{3,2},{4,5},{5,4},{6,7},{7,6},{8,9},{9,8},{10,11... | collective-permute-start | bytes 208904 | tf_op jit(solution)/shard_map/ppermute | solution.py:33
  16.3 6.2 %collective-permute-start.5 = (f32[136,128]{1,0:T(8,128)S(1)}, f32[136,128]{1,0:T(8,128)S(1)}, u32[]{:S(2)}, u32[]{:S(2)}) collective-permute-start(f32[136,128]{1,0:T(8,128)S(1)} %add.34), channel_id=1, source_target_pairs={{0,6},{2,4},{4,2},{6,0},{8,14},{10,12},{12,10},{14,8},{16,22},{18,... | collective-permute-start | bytes 208904 | tf_op jit(solution)/shard_map/ppermute | solution.py:42
  19.1 5.1 %collective-permute-start.4 = (f32[136,128]{1,0:T(8,128)S(1)}, f32[136,128]{1,0:T(8,128)S(1)}, u32[]{:S(2)}, u32[]{:S(2)}) collective-permute-start(f32[136,128]{1,0:T(8,128)S(1)} %add.34), channel_id=1, source_target_pairs={{1,5},{3,7},{5,1},{7,3},{9,13},{11,15},{13,9},{15,11},{17,21},{19,... | collective-permute-start | bytes 208904 | tf_op jit(solution)/shard_map/ppermute | solution.py:43
  24.2 1.3 %collective-permute-start.6 = (f32[136,128]{1,0:T(8,128)S(1)}, f32[136,128]{1,0:T(8,128)S(1)}, u32[]{:S(2)}, u32[]{:S(2)}) collective-permute-start(f32[136,128]{1,0:T(8,128)S(1)} %select_add_fusion.2.mine_ref), channel_id=1, source_target_pairs={{0,1},{1,0},{2,3},{3,2},{4,5},{5,4},{6,7},{7,6},{8,9},{9,8},{10,11... | collective-permute-start | bytes 208904 | tf_op jit(solution)/shard_map/ppermute | solution.py:33
  35.7 7.8 %collective-permute-start.7 = (f32[512,128]{1,0:T(8,128)S(1)}, f32[512,128]{1,0:T(8,128)S(1)}, u32[]{:S(2)}, u32[]{:S(2)}) collective-permute-start(f32[512,128]{1,0:T(8,128)S(1)} %get-tuple-element.4), channel_id=1, source_target_pairs={{224,0},{0,32},{32,64},{64,96},{96,128},{128,160},{160,192},{192,2... | collective-permute-start | bytes 786440 | tf_op jit(solution)/shard_map/ppermute | solution.py:289
  35.8 9.8 %collective-permute-start.8 = (f32[512,128]{1,0:T(8,128)S(1)}, f32[512,128]{1,0:T(8,128)S(1)}, u32[]{:S(2)}, u32[]{:S(2)}) collective-permute-start(f32[512,128]{1,0:T(8,128)S(1)} %get-tuple-element.5), channel_id=1, source_target_pairs={{32,0},{64,32},{96,64},{128,96},{160,128},{192,160},{224,192},{0,2... | collective-permute-start | bytes 786440 | tf_op jit(solution)/shard_map/ppermute | solution.py:289
  45.9 2.1 %collective-permute-start.9 = (f32[136,128]{1,0:T(8,128)S(1)}, f32[136,128]{1,0:T(8,128)S(1)}, u32[]{:S(2)}, u32[]{:S(2)}) collective-permute-start(f32[136,128]{1,0:T(8,128)S(1)} %statistics.1), channel_id=1, source_target_pairs={{0,1},{1,0},{2,3},{3,2},{4,5},{5,4},{6,7},{7,6},{8,9},{9,8},{10,11... | collective-permute-start | bytes 208904 | tf_op jit(solution)/shard_map/ppermute | solution.py:33
  48.0 6.6 %collective-permute-start.11 = (f32[136,128]{1,0:T(8,128)S(1)}, f32[136,128]{1,0:T(8,128)S(1)}, u32[]{:S(2)}, u32[]{:S(2)}) collective-permute-start(f32[136,128]{1,0:T(8,128)S(1)} %add.36), channel_id=1, source_target_pairs={{0,20},{2,22},{4,16},{6,18},{8,28},{10,30},{12,24},{14,26},{16,4},... | collective-permute-start | bytes 208904 | tf_op jit(solution)/shard_map/ppermute | solution.py:42
  50.4 7.2 %collective-permute-start.10 = (f32[136,128]{1,0:T(8,128)S(1)}, f32[136,128]{1,0:T(8,128)S(1)}, u32[]{:S(2)}, u32[]{:S(2)}) collective-permute-start(f32[136,128]{1,0:T(8,128)S(1)} %add.36), channel_id=1, source_target_pairs={{1,25},{3,27},{5,29},{7,31},{9,17},{11,19},{13,21},{15,23},{17,9},... | collective-permute-start | bytes 208904 | tf_op jit(solution)/shard_map/ppermute | solution.py:43
  57.5 1.3 %collective-permute-start.12 = (f32[136,128]{1,0:T(8,128)S(1)}, f32[136,128]{1,0:T(8,128)S(1)}, u32[]{:S(2)}, u32[]{:S(2)}) collective-permute-start(f32[136,128]{1,0:T(8,128)S(1)} %select_add_fusion.1), channel_id=1, source_target_pairs={{0,1},{1,0},{2,3},{3,2},{4,5},{5,4},{6,7},{7,6},{8,9},{9,8},{10,11... | collective-permute-start | bytes 208904 | tf_op jit(solution)/shard_map/ppermute | solution.py:33
  58.9 5.1 %collective-permute-start.14 = (f32[136,128]{1,0:T(8,128)S(1)}, f32[136,128]{1,0:T(8,128)S(1)}, u32[]{:S(2)}, u32[]{:S(2)}) collective-permute-start(f32[136,128]{1,0:T(8,128)S(1)} %add.38), channel_id=1, source_target_pairs={{0,6},{2,4},{4,2},{6,0},{8,14},{10,12},{12,10},{14,8},{16,22},{18,... | collective-permute-start | bytes 208904 | tf_op jit(solution)/shard_map/ppermute | solution.py:42
  60.9 5.0 %collective-permute-start.13 = (f32[136,128]{1,0:T(8,128)S(1)}, f32[136,128]{1,0:T(8,128)S(1)}, u32[]{:S(2)}, u32[]{:S(2)}) collective-permute-start(f32[136,128]{1,0:T(8,128)S(1)} %add.38), channel_id=1, source_target_pairs={{1,5},{3,7},{5,1},{7,3},{9,13},{11,15},{13,9},{15,11},{17,21},{19,... | collective-permute-start | bytes 208904 | tf_op jit(solution)/shard_map/ppermute | solution.py:43
  66.0 1.3 %collective-permute-start.15 = (f32[136,128]{1,0:T(8,128)S(1)}, f32[136,128]{1,0:T(8,128)S(1)}, u32[]{:S(2)}, u32[]{:S(2)}) collective-permute-start(f32[136,128]{1,0:T(8,128)S(1)} %select_add_fusion.mine_ref), channel_id=1, source_target_pairs={{0,1},{1,0},{2,3},{3,2},{4,5},{5,4},{6,7},{7,6},{8,9},{9,8},{10,11... | collective-permute-start | bytes 208904 | tf_op jit(solution)/shard_map/ppermute | solution.py:33
